TPU v7x, 256 devices: a whole 4x4x8 slice. The times are simulated.
256 devices in a mesh: group: 8 (over z), dev: 32 (over y, x, core).
Axes of the slice: x: 4, y: 4, z: 8, core: 2. Of those that a mesh axis runs over, the one named last changes fastest.
Arguments:
- features: bfloat16 [524288, 256], P(('group', 'dev')), may hold values from -6 to 6
- weight_self: bfloat16 [256, 256], replicated, may hold values from -0.375 to 0.375
- weight_neigh: bfloat16 [256, 256], replicated, may hold values from -0.375 to 0.375
- bias: float32 [256], replicated, may hold values from -3 to 3
- cotangent: bfloat16 [524288, 256], P(('group', 'dev')), may hold values from -6 to 6
- hub_rows: int32 [2048], P(('group', 'dev')), may hold values from 0 to 2047, as said below
- halo_send: int32 [8, 32, 32, 128], P('group', 'dev'), may hold values from 0 to 2048, as said below
- block_src: int32 [8, 32, 128], P('group', 'dev'), may hold values from 0 to 63
- block_tgt: int32 [8, 32, 128], P('group', 'dev'), may hold values from 0 to 15
- block_count: int32 [8, 32], P('group', 'dev'), may hold values from 32 to 128, as said below
- block_vals: bfloat16 [8, 32, 128, 128, 128], P('group', 'dev'), may hold values from 0 to 0.071777344
Outputs:
- output: bfloat16 [524288, 256], P(('group', 'dev'))
- grad_features: bfloat16 [524288, 256], P(('group', 'dev'))
- grad_self: float32 [256, 256], replicated
- grad_neigh: float32 [256, 256], replicated
- grad_bias: float32 [256], replicated
Inputs may be any that keep to these rules, and one draw needn't show every extreme that they name: `hub_rows`: the 8 hub rows of one device are distinct. `halo_send`: 2048 marks an empty slot; the rows in one list are distinct and fill its first slots; a device's list to itself is empty. `block_count`: some device has all 128 slots live.
All inputs are finite; a program needn't handle non-finite values.
Results may differ from a plain program's by a relative error of at most 0.0075.
Values may be sent and summed in bfloat16 or wider, within the bound.
A program may use at most 128 MiB of HBM per device.

v0:
```python
import math

import jax
import jax.numpy as jnp
from jax import lax
from jax.sharding import PartitionSpec as P


def silu_parts(pre):
    sigmoid = jax.nn.sigmoid(pre)
    return (pre * sigmoid, sigmoid * (1.0 + pre * (1.0 - sigmoid)))


def shards(
    features,
    weight_self,
    weight_neigh,
    bias,
    cotangent,
    hub_rows,
    halo_send,
    block_src,
    block_tgt,
    block_count,
    block_vals,
):
    rows_here = features.shape[0]
    width = features.shape[1]
    peers_count = lax.axis_size("dev")
    nodes = rows_here * lax.axis_size("group") * peers_count
    scale = 1.0 / math.sqrt(nodes)
    contract = (((0,), (0,)), ((), ()))
    contract_last = (((1,), (1,)), ((), ()))
    send_lists = halo_send[0, 0]
    padded = jnp.concatenate([features, jnp.zeros((1, width), jnp.bfloat16)], axis=0)
    outgoing = padded[send_lists]
    halo = lax.all_to_all(outgoing, "dev", split_axis=0, concat_axis=0, tiled=True)
    mine = features[hub_rows]
    hubs = lax.all_gather(mine, ("group", "dev"), axis=0, tiled=True)
    table = jnp.concatenate([features, halo.reshape(-1, width), hubs], axis=0)
    values = block_vals[0, 0]
    block = values.shape[-1]
    capacity = values.shape[0]
    tiles = table.reshape(-1, block, width)
    src_blocks = tiles.shape[0]
    target_blocks = rows_here // block
    sources = block_src[0, 0]
    targets = block_tgt[0, 0]
    live = jnp.arange(capacity) < block_count[0, 0]
    masked = jnp.where(live[:, None, None], values, jnp.zeros((), jnp.bfloat16))
    products = jnp.einsum(
        "kij,kjf->kif", masked, tiles[sources], preferred_element_type=jnp.float32
    )
    aggregated = jax.ops.segment_sum(products, targets, num_segments=target_blocks)
    aggregated = aggregated.reshape(rows_here, width).astype(jnp.bfloat16)
    pre = (
        jnp.dot(features, weight_self, preferred_element_type=jnp.float32)
        + jnp.dot(aggregated, weight_neigh, preferred_element_type=jnp.float32)
        + bias
    )
    output, slope = silu_parts(pre)
    dpre = (cotangent.astype(jnp.float32) * slope).astype(jnp.bfloat16)
    grad_self = lax.dot_general(features, dpre, contract, preferred_element_type=jnp.float32)
    grad_neigh = lax.dot_general(aggregated, dpre, contract, preferred_element_type=jnp.float32)
    grad_bias = jnp.sum(dpre.astype(jnp.float32), axis=0)
    summed_self, summed_neigh, summed_bias = lax.psum(
        (grad_self, grad_neigh, grad_bias), ("group", "dev")
    )
    dagg = lax.dot_general(
        dpre, weight_neigh, contract_last, preferred_element_type=jnp.float32
    ).astype(jnp.bfloat16)
    dagg_tiles = dagg.reshape(target_blocks, block, width)[targets]
    back = jnp.einsum("kji,kjf->kif", masked, dagg_tiles, preferred_element_type=jnp.float32)
    dtable = jax.ops.segment_sum(back, sources, num_segments=src_blocks)
    dtable = dtable.reshape(-1, width)
    hub_start = rows_here + peers_count * block
    halo_back = dtable[rows_here:hub_start].astype(jnp.bfloat16).reshape(peers_count, block, width)
    returned = lax.all_to_all(halo_back, "dev", split_axis=0, concat_axis=0, tiled=True)
    hub_part = dtable[hub_start:]
    hub_sums = lax.psum_scatter(hub_part, ("group", "dev"), scatter_dimension=0, tiled=True)
    local = (
        lax.dot_general(dpre, weight_self, contract_last, preferred_element_type=jnp.float32)
        + dtable[:rows_here]
    )
    grads = jnp.concatenate([local, jnp.zeros((1, width), jnp.float32)], axis=0)
    grads = grads.at[send_lists.reshape(-1)].add(returned.reshape(-1, width).astype(jnp.float32))
    grads = grads.at[hub_rows].add(hub_sums)
    grad_features = grads[:rows_here].astype(jnp.bfloat16)
    return (
        output.astype(jnp.bfloat16),
        grad_features,
        summed_self * scale,
        summed_neigh * scale,
        summed_bias * scale,
    )


def solution(mesh):
    return jax.shard_map(
        shards,
        mesh=mesh,
        in_specs=(
            P(("group", "dev"), None),
            P(),
            P(),
            P(),
            P(("group", "dev"), None),
            P(("group", "dev")),
            P("group", "dev", None, None),
            P("group", "dev", None),
            P("group", "dev", None),
            P("group", "dev"),
            P("group", "dev", None, None, None),
        ),
        out_specs=(P(("group", "dev"), None), P(("group", "dev"), None), P(), P(), P()),
        check_vma=False,
    )
```

profile of v0, /device:TPU:1, one launch (start us, length us, event | category | flops | bytes accessed | tf_op | source)
XLA Modules:
  0.0 1727.5 jit_solution(13023866689237027088)
XLA Ops:
  7.9 2.5 gather_fusion.1
  12.5 16.9 gather_fusion
  29.4 8.7 all-to-all-start
  39.0 1.8 fusion.12
  40.8 25.3 %all-to-all-done = bf16[32,128,256]{2,1,0:T(8,128)(2,1)S(1)} async-done(((bf16[32,128,256]{2,1,0:T(8,128)(2,1)}), bf16[32,128,256]{2,1,0:T(8,128)(2,1)S(1)}, u32[]{:S(2)}, u32[]{:S(2)}) %all-to-all-start) | async-done | bytes 2097184 | tf_op jit(solution)/shard_map/all_to_all | solution.py:37
  66.1 54.4 %all-gather.3.cloned.1.call-done = bf16[2048,256]{1,0:T(8,128)(2,1)} async-done(((bf16[8,256]{1,0:T(8,128)(2,1)}), bf16[2048,256]{1,0:T(8,128)(2,1)}) %all-gather.3.cloned.1.call-update) | async-done | bytes 1048592 | tf_op jit(solution)/shard_map/all_gather | solution.py:39
  120.5 3.1 pad_maximum_fusion
  123.7 8.8 gather_fusion.2
  132.4 12.8 fusion.4
  145.4 24.3 %scatter_fusion = f32[16,128,256]{2,1,0:T(8,128)S(1)} fusion(f32[16,128,256]{2,1,0:T(8,128)S(1)} %broadcast_in_dim.32, s32[128]{0:T(128)S(1)} %bitcast.59, f32[128,128,256]{2,1,0:T(8,128)} %fusion.4), kind=kCustom, calls=%fused_computation.4 | custom fusion | flops 4194304 | bytes 50332160 | tf_op jit(solution)/shard_map/scatter-add | solution.py:54
  169.9 4.1 convert_reduce_fusion
  176.9 6.6 gather_fusion.3
  183.5 13.9 fusion.3
  197.4 4.2 broadcast_in_dim.36
  201.7 38.8 %scatter_fusion.1 = f32[64,128,256]{2,1,0:T(8,128)} fusion(f32[64,128,256]{2,1,0:T(8,128)} %broadcast_in_dim.36, s32[128]{0:T(128)S(1)} %bitcast.60, f32[128,128,256]{2,1,0:T(8,128)} %fusion.3), kind=kCustom, calls=%fused_computation.5 | custom fusion | flops 4194304 | bytes 50332160 | tf_op jit(solution)/shard_map/scatter-add | solution.py:74
  240.5 4.7 fusion.11
  245.2 3.8 slice.41
  249.0 6.8 all-to-all-start.1
  255.8 2.1 convolution_add_fusion
  258.0 91.9 %psum.23 = f32[256]{0:T(256)S(1)} all-reduce(f32[256]{0:T(256)S(1)} %get-tuple-element.12), channel_id=1, replica_groups=mesh['group'=8,'dev'=32] {'group','dev'}, use_global_device_ids=true, to_apply=%region_8.9 | all-reduce | flops 256 | bytes 2048 | tf_op jit(solution)/shard_map/psum | solution.py:66
  350.5 98.8 %all-reduce.5.cloned.1.call-done = (f32[256,256]{0,1:T(8,128)}, f32[256,256]{0,1:T(8,128)}) async-done(((f32[256,256]{0,1:T(8,128)}, f32[256,256]{0,1:T(8,128)}), (f32[256,256]{0,1:T(8,128)}, f32[256,256]{0,1:T(8,128)})) %all-reduce.5.cloned.1.call-update) | async-done | bytes 524304 | tf_op jit(solution)/shard_map/psum | solution.py:66
  452.1 25.4 %scatter_custom_fusion.2 = f32[2049,256]{1,0:T(8,128)S(1)} fusion(f32[2049,256]{1,0:T(8,128)S(1)} %concatenate.11, s32[4096]{0:T(1024)S(1)} %bitcast.58, bf16[4096,256]{1,0:T(8,128)(2,1)} %bitcast.21), kind=kCustom, calls=%fused_computation.10 | custom fusion | flops 2097152 | bytes 4195328 | tf_op jit(solution)/shard_map/scatter-add | solution.py:86
  477.5 1240.9 %reduce-scatter.2.cloned.1.call-done = f32[8,256]{1,0:T(8,128)} async-done(((f32[2048,256]{1,0:T(8,128)}), f32[8,256]{1,0:T(8,128)}) %reduce-scatter.2.cloned.1.call-update) | async-done | bytes 8208 | tf_op jit(solution)/shard_map/reduce_scatter | solution.py:80
  1718.4 1.5 scatter_fusion.2
  (44 shorter events, 10.7 us)
Async XLA Ops:
  7.2 162.7 %copy-start = (bf16[256,256]{1,0:T(8,128)(2,1)S(1)}, bf16[256,256]{1,0:T(8,128)(2,1)}, u32[]{:S(2)}) copy-start(bf16[256,256]{1,0:T(8,128)(2,1)} %param.13) | copy-start | bytes 393220
  7.2 113.4 %all-gather.3.cloned.1.call-start = ((), (), s32[]{:S(2)}) async-start(), calls=%async_computation.4 | async-start | bytes 1052672 | tf_op jit(solution)/shard_map/all_gather | solution.py:39
  29.4 9.5 copy-start.6
  29.4 9.5 copy-start.5
  29.4 9.5 copy-start.2
  29.4 9.5 copy-start.3
  29.4 36.7 %all-to-all-start = ((bf16[32,128,256]{2,1,0:T(8,128)(2,1)}), bf16[32,128,256]{2,1,0:T(8,128)(2,1)S(1)}, u32[]{:S(2)}, u32[]{:S(2)}) async-start(bf16[32,128,256]{2,1,0:T(8,128)(2,1)} %bitcast.54), calls=%async_computation | async-start | bytes 4194304 | tf_op jit(solution)/shard_map/all_to_all | solution.py:37
  38.2 411.1 %all-reduce.5.cloned.1.call-start = ((), (), s32[]{:S(2)}) async-start(), calls=%async_computation.5 | async-start | bytes 1048576 | tf_op jit(solution)/shard_map/psum | solution.py:66
  145.4 24.5 %copy-start.7 = (f32[256]{0:T(256)S(1)}, f32[256]{0:T(256)}, u32[]{:S(2)}) copy-start(f32[256]{0:T(256)} %param.14) | copy-start | bytes 3076
  197.4 1521.0 %reduce-scatter.2.cloned.1.call-start = ((), (), s32[]{:S(2)}) async-start(), calls=%async_computation.3 | async-start | bytes 2105344 | tf_op jit(solution)/shard_map/reduce_scatter | solution.py:80
  245.2 10.6 copy-start.4
  249.0 203.1 %all-to-all-start.1 = ((bf16[32,128,256]{2,1,0:T(8,128)(2,1)}), bf16[32,128,256]{2,1,0:T(8,128)(2,1)}, u32[]{:S(2)}, u32[]{:S(2)}) async-start(bf16[32,128,256]{2,1,0:T(8,128)(2,1)} %slice.41), calls=%async_computation.1 | async-start | bytes 4194304 | tf_op jit(solution)/shard_map/all_to_all | solution.py:78
  449.3 1271.7 %copy-start.1 = (bf16[256,256]{1,0:T(8,128)(2,1)S(1)}, bf16[256,256]{1,0:T(8,128)(2,1)}, u32[]{:S(2)}) copy-start(bf16[256,256]{1,0:T(8,128)(2,1)} %param.13) | copy-start | bytes 393220
Sparse Core Ops, SparseCore 0:
  12.3 108.1 all-gather.2
  197.5 251.7 all-reduce.4
  451.8 1266.5 reduce-scatter.1
where the time goes:
time: 1730 us
  waiting for transfers between devices  1420 us (82%)
  other arithmetic  96.5 us (6%)
  blocking collectives  91.9 us (5%)
  local copies, waits for them, and re-layouts  51.9 us (3%)
  matrix products  37.5 us (2%)
    reduce_scatter x1, waiting for transfers between devices, shards(): lax.psum_scatter(hub_part, ('group', 'dev'), scatter_dimension=0, tiled=T...  1240 us
    psum x1, waiting for transfers between devices, shards(): lax.psum((grad_self, grad_neigh, grad_bias), ('group', 'dev'))  98.8 us
    psum x1, blocking collectives, shards(): lax.psum((grad_self, grad_neigh, grad_bias), ('group', 'dev'))  91.9 us
    all_gather x1, waiting for transfers between devices, shards(): hubs = lax.all_gather(mine, ('group', 'dev'), axis=0, tiled=True)  54.4 us
    scatter-add x1, other arithmetic, shards(): dtable = jax.ops.segment_sum(back, sources, num_segments=src_blocks)  38.8 us
  transfers between devices with their start and end apart: 5, of which 4 were waited for; matrix products, arithmetic and copies ran while one was open for 6% of the time, Pallas kernels for 0%

commit v1 on v0

v1 whole, which is shorter than its diff:
```python
import functools
import math

import jax
import jax.numpy as jnp
from jax import lax
from jax.experimental import pallas as pl
from jax.experimental.pallas import tpu as pltpu
from jax.sharding import PartitionSpec as P

MESH = pl.DeviceIdType.MESH
LANES = 128
BF16 = jnp.bfloat16
F32 = jnp.float32
FIRST = (((0,), (0,)), ((), ()))
LAST = (((1,), (1,)), ((), ()))
MIB = 1 << 20


def partner(me, step):
    core = lax.rem(lax.rem(me, 2) + lax.rem(step, 2), 2)
    x = lax.rem(lax.div(me, 2) + lax.div(step, 2), 4)
    y = lax.div(me, 8) + lax.div(step, 8)
    return x * 2 + core, y


def peer_of(me, step, count):
    low, y = partner(me, step)
    return lax.rem(y, count // 8) * 8 + low


def greet(me, group, devs, groups):
    barrier = pltpu.get_barrier_semaphore()

    def plane(step, _):
        pl.semaphore_signal(
            barrier, inc=1, device_id={"dev": peer_of(me, step, devs)}, device_id_type=MESH
        )
        return _

    def column(step, _):
        pl.semaphore_signal(
            barrier, inc=1, device_id={"group": lax.rem(group + step, groups)}, device_id_type=MESH
        )
        return _

    lax.fori_loop(1, devs, plane, 0)
    lax.fori_loop(1, groups, column, 0)
    return barrier


def to_plane(src, dst, send, recv, peer):
    return pltpu.make_async_remote_copy(
        src_ref=src, dst_ref=dst, send_sem=send, recv_sem=recv,
        device_id={"dev": peer}, device_id_type=MESH,
    )


def to_column(src, dst, send, recv, peer):
    return pltpu.make_async_remote_copy(
        src_ref=src, dst_ref=dst, send_sem=send, recv_sem=recv,
        device_id={"group": peer}, device_id_type=MESH,
    )


def gather_kernel(
    groups, devs,
    feat, lists, hub_idx,
    halo, hubs,
    out_buf, hub_out, hub_in, hub_own,
    sends, recvs, hub_sends, hub_recvs, z_sends, z_recvs, c_sends, c_recvs, local_sem,
):
    group = lax.axis_index("group")
    me = lax.axis_index("dev")
    rows, width = feat.shape
    slots = lists.shape[1]
    share = hub_out.shape[0]
    plane_hubs = share * devs
    half = plane_hubs // 2
    core = lax.rem(me, 2)
    mate = me + 1 - 2 * core
    barrier = greet(me, group, devs, groups)

    lane = lax.broadcasted_iota(jnp.int32, (slots, LANES), 1)

    def onehot(column, ids):
        return jnp.concatenate(
            [
                jnp.where(column == ids + LANES * r, 1.0, 0.0).astype(BF16)
                for r in range(rows // LANES)
            ],
            axis=1,
        )

    picked = jnp.dot(
        onehot(hub_idx[...], lane[: hub_idx.shape[0]]), feat[...], preferred_element_type=F32
    )[:share]
    hub_out[...] = picked
    hub_in[pl.ds(pl.multiple_of(me * share, share), share), :] = picked

    def fill(chunk):
        parts = []
        for j in range(4):
            row = lists[pl.ds(peer_of(me, chunk * 4 + j, devs), 1), :]
            column = jnp.broadcast_to(row, (slots, slots)).T
            parts.append(onehot(column, lane))
        got = jnp.dot(jnp.concatenate(parts, axis=0), feat[...], preferred_element_type=F32)
        out_buf[pl.ds(chunk * 4, 4)] = got.astype(BF16).reshape(4, slots, width)

    fill(0)
    pl.semaphore_wait(barrier, devs + groups - 2)

    def hub_copy(step):
        peer = peer_of(me, step, devs)
        place = pl.ds(pl.multiple_of(me * share, share), share)
        return to_plane(hub_out, hub_in.at[place], hub_sends.at[step], hub_recvs.at[me], peer)

    def halo_copy(step):
        peer = peer_of(me, step, devs)
        return to_plane(out_buf.at[step], halo.at[me], sends.at[step], recvs.at[me], peer)

    def each(low, high, action):
        def body(step, _):
            action(step)
            return _
        lax.fori_loop(low, high, body, 0)

    each(1, devs, lambda step: hub_copy(step).start())
    own = pltpu.make_async_copy(out_buf.at[0], halo.at[me], local_sem.at[0])
    own.start()
    each(1, 4, lambda step: halo_copy(step).start())

    def later(chunk):
        fill(chunk)
        each(chunk * 4, chunk * 4 + 4, lambda step: halo_copy(step).start())

    each(1, devs // 4, later)

    def hub_arrived(step):
        peer = peer_of(me, step, devs)
        place = pl.ds(pl.multiple_of(peer * share, share), share)
        to_plane(hub_out, hub_in.at[place], hub_sends.at[step], hub_recvs.at[peer], peer).wait_recv()

    each(1, devs, hub_arrived)
    hub_own[...] = hub_in[...].astype(BF16)
    mine = pltpu.make_async_copy(
        hub_own, hubs.at[pl.ds(pl.multiple_of(group * plane_hubs, plane_hubs), plane_hubs)], local_sem.at[1]
    )
    mine.start()

    def half_of(which, side):
        return pl.ds(pl.multiple_of(which * plane_hubs + side * half, half), half)

    def z_copy(step):
        part = hub_own.at[pl.ds(pl.multiple_of(core * half, half), half)]
        return to_column(
            part, hubs.at[half_of(group, core)], z_sends.at[step], z_recvs.at[group],
            lax.rem(group + step, groups),
        )

    each(1, groups, lambda step: z_copy(step).start())

    def z_arrived(step):
        source = lax.rem(group + groups - step, groups)
        part = hubs.at[half_of(source, core)]
        to_column(part, part, z_sends.at[step], z_recvs.at[source], source).wait_recv()
        to_plane(part, part, c_sends.at[source], c_recvs.at[source], mate).start()

    each(1, groups, z_arrived)

    def c_done(step):
        source = lax.rem(group + groups - step, groups)
        out = hubs.at[half_of(source, core)]
        into = hubs.at[half_of(source, 1 - core)]
        to_plane(out, out, c_sends.at[source], c_recvs.at[source], mate).wait_send()
        to_plane(into, into, c_sends.at[source], c_recvs.at[source], mate).wait_recv()

    each(1, groups, c_done)
    each(1, groups, lambda step: z_copy(step).wait_send())
    each(1, devs, lambda step: hub_copy(step).wait_send())

    def halo_done(step):
        peer = peer_of(me, step, devs)
        to_plane(out_buf.at[step], halo.at[peer], sends.at[step], recvs.at[peer], peer).wait()

    each(1, devs, halo_done)
    own.wait()
    mine.wait()


def gather_call(features, lists, hub_idx, groups, devs, share):
    rows, width = features.shape
    slots = lists.shape[1]
    hubs = groups * devs * share
    dma = pltpu.SemaphoreType.DMA
    return pl.pallas_call(
        functools.partial(gather_kernel, groups, devs),
        out_shape=(
            jax.ShapeDtypeStruct((devs, slots, width), BF16),
            jax.ShapeDtypeStruct((hubs, width), BF16),
        ),
        in_specs=[pl.BlockSpec(memory_space=pltpu.VMEM)] * 3,
        out_specs=[pl.BlockSpec(memory_space=pl.ANY)] * 2,
        scratch_shapes=[
            pltpu.VMEM((devs, slots, width), BF16),
            pltpu.VMEM((share, width), F32),
            pltpu.VMEM((devs * share, width), F32),
            pltpu.VMEM((devs * share, width), BF16),
            dma((devs,)), dma((devs,)), dma((devs,)), dma((devs,)),
            dma((groups,)), dma((groups,)), dma((groups,)), dma((groups,)), dma((2,)),
        ],
        compiler_params=pltpu.CompilerParams(
            collective_id=0, has_side_effects=True, vmem_limit_bytes=24 * MIB
        ),
        name="halo_gather",
    )(features, lists, hub_idx)


UNROLL = 4


def layer_kernel(
    src, tgt, count,
    feat, halo, hubs, vals, ws, wn, bias, cot,
    output, halo_back, hub_back, own_back, dpre_ref, wsend,
    table, agg, aggb, dagg, dtab, gself, gneigh, gbias, sems,
):
    blocks, block, width = table.shape
    capacity = vals.shape[0]
    own_blocks = feat.shape[0] // block
    halo_blocks = halo.shape[0]
    copies = [
        pltpu.make_async_copy(halo, table.at[pl.ds(own_blocks, halo_blocks)], sems.at[0]),
        pltpu.make_async_copy(
            hubs, table.at[pl.ds(own_blocks + halo_blocks, blocks - own_blocks - halo_blocks)], sems.at[1]
        ),
    ]
    for copy in copies:
        copy.start()
    agg[...] = jnp.zeros_like(agg)
    dtab[...] = jnp.zeros_like(dtab)
    gself[...] = jnp.zeros_like(gself)
    gneigh[...] = jnp.zeros_like(gneigh)
    gbias[...] = jnp.zeros_like(gbias)
    table[pl.ds(0, own_blocks)] = feat[...].reshape(own_blocks, block, width)
    for copy in copies:
        copy.wait()
    live = count[0]
    steps = lax.div(live + UNROLL - 1, UNROLL)

    def value(k):
        return jnp.where(k < live, vals[k], jnp.zeros((), BF16))

    def forward(step, _):
        for u in range(UNROLL):
            k = step * UNROLL + u
            agg[tgt[k]] += jnp.dot(value(k), table[src[k]], preferred_element_type=F32)
        return _

    lax.fori_loop(0, steps, forward, 0)

    def dense(t, _):
        at = pl.ds(pl.multiple_of(t * 2 * block, 2 * block), 2 * block)
        own = feat[at, :]
        two = pl.ds(t * 2, 2)
        near = agg[two].reshape(2 * block, width).astype(BF16)
        aggb[at, :] = near
        pre = (
            jnp.dot(own, ws[...], preferred_element_type=F32)
            + jnp.dot(near, wn[...], preferred_element_type=F32)
            + bias[...]
        )
        sigmoid = jax.nn.sigmoid(pre)
        output[at, :] = (pre * sigmoid).astype(BF16)
        slope = sigmoid * (1.0 + pre * (1.0 - sigmoid))
        dpre = (cot[at, :].astype(F32) * slope).astype(BF16)
        dpre_ref[at, :] = dpre
        dagg[two] = (
            lax.dot_general(dpre, wn[...], LAST, preferred_element_type=F32)
            .astype(BF16)
            .reshape(2, block, width)
        )
        gself[...] += lax.dot_general(own, dpre, FIRST, preferred_element_type=F32)
        gneigh[...] += lax.dot_general(near, dpre, FIRST, preferred_element_type=F32)
        gbias[...] += jnp.sum(dpre.astype(F32), axis=0, keepdims=True)
        return _

    lax.fori_loop(0, own_blocks // 2, dense, 0)

    def backward(step, _):
        for u in range(UNROLL):
            k = step * UNROLL + u
            dtab[src[k]] += lax.dot_general(
                value(k), dagg[tgt[k]], FIRST, preferred_element_type=F32
            )
        return _

    lax.fori_loop(0, steps, backward, 0)

    own_back[...] = dtab[pl.ds(0, own_blocks)].reshape(own_blocks * block, width)

    def rounded(p, _):
        halo_back[p] = dtab[own_blocks + p].astype(BF16)
        return _

    lax.fori_loop(0, halo_blocks, rounded, 0)

    hub_blocks = blocks - own_blocks - halo_blocks
    hub_back[...] = (
        dtab[pl.ds(own_blocks + halo_blocks, hub_blocks)].astype(BF16).reshape(hub_back.shape)
    )
    parts = wsend.shape[0]
    rows = 2 * width // parts
    wsend[pl.ds(0, parts // 2), :, pl.ds(0, width)] = gself[...].astype(BF16).reshape(
        parts // 2, rows, width
    )
    wsend[pl.ds(parts // 2, parts // 2), :, pl.ds(0, width)] = gneigh[...].astype(BF16).reshape(
        parts // 2, rows, width
    )
    line = lax.broadcasted_iota(jnp.int32, (rows, LANES), 0)
    low, high = gbias[:, :LANES], gbias[:, LANES:]
    both = jnp.where(line == 0, low, jnp.where(line == 1, high, 0.0))
    wsend[:, :, pl.ds(width, LANES)] = jnp.broadcast_to(
        both.astype(BF16)[None], (parts, rows, LANES)
    )


def layer_call(src, tgt, count, features, halo, hubs, values, ws, wn, bias, cot, groups, devs):
    rows, width = features.shape
    block = values.shape[1]
    own_blocks = rows // block
    blocks = own_blocks + devs + hubs.shape[0] // block
    half = hubs.shape[0] // groups // 2
    vmem = pl.BlockSpec(memory_space=pltpu.VMEM)
    smem = pl.BlockSpec(memory_space=pltpu.SMEM)
    anywhere = pl.BlockSpec(memory_space=pl.ANY)
    return pl.pallas_call(
        layer_kernel,
        out_shape=(
            jax.ShapeDtypeStruct((rows, width), BF16),
            jax.ShapeDtypeStruct((devs, block, width), BF16),
            jax.ShapeDtypeStruct((groups, 2, half, width), BF16),
            jax.ShapeDtypeStruct((rows, width), F32),
            jax.ShapeDtypeStruct((rows, width), BF16),
            jax.ShapeDtypeStruct((devs, 2 * width // devs, width + LANES), BF16),
        ),
        in_specs=[smem] * 3 + [vmem, anywhere, anywhere] + [vmem] * 5,
        out_specs=[vmem] * 6,
        scratch_shapes=[
            pltpu.VMEM((blocks, block, width), BF16),
            pltpu.VMEM((own_blocks, block, width), F32),
            pltpu.VMEM((rows, width), BF16),
            pltpu.VMEM((own_blocks, block, width), BF16),
            pltpu.VMEM((blocks, block, width), F32),
            pltpu.VMEM((width, width), F32),
            pltpu.VMEM((width, width), F32),
            pltpu.VMEM((1, width), F32),
            pltpu.SemaphoreType.DMA((2,)),
        ],
        compiler_params=pltpu.CompilerParams(vmem_limit_bytes=48 * MIB),
        name="layer",
    )(src, tgt, count, features, halo, hubs.reshape(-1, block, width), values, ws, wn, bias, cot)


def return_kernel(
    groups, devs,
    lists, hub_idx, halo_back, hub_back, own_back, dpre, ws, wsend,
    grad, wout, bias_out,
    acc, halo_in, pair_in, z_out, z_in, row_out, row_in, w_in, wz_in, wfin,
    h_send, h_recv, p_sem, z_send, z_recv, r_send, r_recv,
    w_send, w_recv, y_send, y_recv, f_send, f_recv,
):
    group = lax.axis_index("group")
    me = lax.axis_index("dev")
    rows, width = grad.shape
    slots = lists.shape[1]
    core = lax.rem(me, 2)
    mate = me + 1 - 2 * core
    share = row_out.shape[1]
    owners = row_out.shape[0]
    barrier = greet(me, group, devs, groups)

    def each(low, high, action):
        def body(step, _):
            action(step)
            return _
        lax.fori_loop(low, high, body, 0)

    def w_copy(step):
        peer = peer_of(me, step, devs)
        return to_plane(wsend.at[peer], w_in.at[me], w_send.at[step], w_recv.at[me], peer)

    def halo_copy(step):
        peer = peer_of(me, step, devs)
        return to_plane(halo_back.at[peer], halo_in.at[me], h_send.at[step], h_recv.at[me], peer)

    pair = to_plane(hub_back.at[:, 1 - core], pair_in, p_sem.at[0], p_sem.at[1], mate)

    pl.semaphore_wait(barrier, devs + groups - 2)
    pair.start()
    each(1, devs, lambda step: w_copy(step).start())
    each(1, devs, lambda step: halo_copy(step).start())

    w_in[me] = wsend[me]
    halo_in[me] = jnp.zeros((slots, width), BF16)

    def begin(t):
        at = pl.ds(pl.multiple_of(t * 256, 256), 256)
        acc[at, :] = (
            lax.dot_general(dpre[at, :], ws[...], LAST, preferred_element_type=F32) + own_back[at, :]
        )

    each(0, rows // 256, begin)

    pair.wait_recv()
    z_out[...] = (hub_back[:, core].astype(F32) + pair_in[...].astype(F32)).astype(BF16)

    def z_copy(step):
        peer = lax.rem(group + step, groups)
        return to_column(z_out.at[peer], z_in.at[group], z_send.at[step], z_recv.at[group], peer)

    each(1, groups, lambda step: z_copy(step).start())
    z_in[group] = z_out[group]

    def w_arrived(step):
        peer = peer_of(me, step, devs)
        to_plane(wsend.at[peer], w_in.at[peer], w_send.at[step], w_recv.at[peer], peer).wait_recv()

    each(1, devs, w_arrived)
    wz_in[group] = jnp.sum(w_in[...].astype(F32), axis=0).astype(BF16)

    def y_copy(step):
        peer = lax.rem(group + step, groups)
        return to_column(wz_in.at[group], wz_in.at[group], y_send.at[step], y_recv.at[group], peer)

    each(1, groups, lambda step: y_copy(step).start())

    def scatter(chunk):
        wide = 4 * slots
        ids = []
        got = []
        for j in range(4):
            step = chunk * 4 + j
            peer = peer_of(me, step, devs)

            @pl.when(step > 0)
            def _():
                to_plane(
                    halo_back.at[peer], halo_in.at[peer], h_send.at[step], h_recv.at[peer], peer
                ).wait_recv()

            ids.append(lists[pl.ds(peer, 1), :])
            got.append(halo_in[peer])
        ids = jnp.concatenate(ids, axis=1)
        got = jnp.concatenate(got, axis=0)
        for t in range(rows // 256):
            node = lax.broadcasted_iota(jnp.int32, (256, wide), 0) + t * 256
            pick = jnp.where(node == ids, 1.0, 0.0).astype(BF16)
            acc[pl.ds(t * 256, 256), :] += jnp.dot(pick, got, preferred_element_type=F32)

    def y_arrived(step):
        peer = lax.rem(group + step, groups)
        to_column(
            wz_in.at[peer], wz_in.at[peer], y_send.at[step], y_recv.at[peer], peer
        ).wait_recv()

    each(1, groups, y_arrived)
    total = jnp.sum(wz_in[...].astype(F32), axis=0)
    wfin[me] = total[:, :width].astype(BF16)
    bias_out[...] = total[:8, width:]

    def f_copy(step):
        peer = peer_of(me, step, devs)
        return to_plane(wfin.at[me], wfin.at[me], f_send.at[step], f_recv.at[me], peer)

    each(1, devs, lambda step: f_copy(step).start())

    def z_arrived(step):
        peer = lax.rem(group + step, groups)
        to_column(z_out.at[peer], z_in.at[peer], z_send.at[step], z_recv.at[peer], peer).wait_recv()

    each(1, groups, z_arrived)
    row_out[...] = jnp.sum(z_in[...].astype(F32), axis=0).reshape(owners, share, width)

    chip = lax.div(me, 2)

    def row_copy(k):
        owner = core * owners + k
        return to_plane(row_out.at[k], row_in.at[chip], r_send.at[k], r_recv.at[chip], owner)

    def row_start(k):
        owner = core * owners + k

        @pl.when(owner != me)
        def _():
            row_copy(k).start()

        @pl.when(owner == me)
        def _():
            row_in[chip] = row_out[k]

    each(0, owners, row_start)

    each(0, devs // 4, scatter)

    side = lax.div(me, owners)

    def row_arrived(k):
        sender = k * 2 + side

        @pl.when(sender != me)
        def _():
            to_plane(row_out.at[k], row_in.at[k], r_send.at[k], r_recv.at[k], sender).wait_recv()

    each(0, owners, row_arrived)
    total = jnp.sum(row_in[...], axis=0)
    top = total.astype(BF16)
    rest = (total - top.astype(F32)).astype(BF16)
    both = jnp.concatenate([top.astype(F32), rest.astype(F32)], axis=0).astype(BF16)
    for t in range(rows // 256):
        node = lax.broadcasted_iota(jnp.int32, (256, 2 * share), 0) + t * 256
        pick = jnp.where(node == hub_idx[...], 1.0, 0.0).astype(BF16)
        at = pl.ds(t * 256, 256)
        grad[at, :] = (
            acc[at, :] + jnp.dot(pick, both, preferred_element_type=F32)
        ).astype(BF16)

    def f_arrived(step):
        peer = peer_of(me, step, devs)
        to_plane(wfin.at[peer], wfin.at[peer], f_send.at[step], f_recv.at[peer], peer).wait_recv()

    each(1, devs, f_arrived)
    wout[...] = wfin[...]

    def sent(step):
        w_copy(step).wait_send()
        halo_copy(step).wait_send()
        f_copy(step).wait_send()

    each(1, devs, sent)

    def column_sent(step):
        z_copy(step).wait_send()
        y_copy(step).wait_send()

    each(1, groups, column_sent)

    def row_sent(k):
        @pl.when(core * owners + k != me)
        def _():
            row_copy(k).wait_send()

    each(0, owners, row_sent)
    pair.wait_send()


def return_call(lists, hub_idx, halo_back, hub_back, own_back, dpre, ws, wsend, groups, devs, share):
    rows, width = dpre.shape
    slots = lists.shape[1]
    half = hub_back.shape[2]
    owners = half // share
    wrows = wsend.shape[1]
    dma = pltpu.SemaphoreType.DMA
    vmem = pl.BlockSpec(memory_space=pltpu.VMEM)
    anywhere = pl.BlockSpec(memory_space=pl.ANY)
    return pl.pallas_call(
        functools.partial(return_kernel, groups, devs),
        out_shape=(
            jax.ShapeDtypeStruct((rows, width), BF16),
            jax.ShapeDtypeStruct((devs, wrows, width), BF16),
            jax.ShapeDtypeStruct((8, LANES), F32),
        ),
        in_specs=[vmem, vmem, anywhere, vmem, vmem, vmem, vmem, vmem],
        out_specs=[vmem] * 3,
        scratch_shapes=[
            pltpu.VMEM((rows, width), F32),
            pltpu.VMEM((devs, slots, width), BF16),
            pltpu.VMEM((groups, half, width), BF16),
            pltpu.VMEM((groups, half, width), BF16),
            pltpu.VMEM((groups, half, width), BF16),
            pltpu.VMEM((owners, share, width), F32),
            pltpu.VMEM((devs // 2, share, width), F32),
            pltpu.VMEM((devs, wrows, width + LANES), BF16),
            pltpu.VMEM((groups, wrows, width + LANES), BF16),
            pltpu.VMEM((devs, wrows, width), BF16),
            dma((devs,)), dma((devs,)), dma((2,)), dma((groups,)), dma((groups,)),
            dma((owners,)), dma((devs // 2,)),
            dma((devs,)), dma((devs,)), dma((groups,)), dma((groups,)), dma((devs,)), dma((devs,)),
        ],
        compiler_params=pltpu.CompilerParams(
            collective_id=1, has_side_effects=True, vmem_limit_bytes=40 * MIB
        ),
        name="halo_return",
    )(lists, hub_idx, halo_back, hub_back, own_back, dpre, ws, wsend)


def shards(groups, devs, features, weight_self, weight_neigh, bias, cotangent, hub_rows,
           halo_send, block_src, block_tgt, block_count, block_vals):
    rows, width = features.shape
    scale = 1.0 / math.sqrt(rows * groups * devs)
    share = hub_rows.shape[0]
    lists = halo_send[0, 0]
    doubled = jnp.concatenate([hub_rows, hub_rows])
    columns = jnp.broadcast_to(doubled[:, None], (2 * share, LANES))
    halo, hubs = gather_call(features, lists, columns, groups, devs, share)
    output, halo_back, hub_back, own_back, dpre, wsend = layer_call(
        block_src[0, 0], block_tgt[0, 0], block_count[0], features, halo, hubs, block_vals[0, 0],
        weight_self, weight_neigh, bias[None], cotangent, groups, devs,
    )
    grad, wout, bias_out = return_call(
        lists, doubled[None], halo_back, hub_back, own_back, dpre, weight_self, wsend,
        groups, devs, share,
    )
    wgrad = wout.reshape(2, width, width).astype(F32) * scale
    return output, grad, wgrad[0], wgrad[1], bias_out[:2].reshape(width) * scale


def solution(mesh):
    groups, devs = mesh.shape["group"], mesh.shape["dev"]
    return jax.shard_map(
        functools.partial(shards, groups, devs),
        mesh=mesh,
        in_specs=(
            P(("group", "dev"), None),
            P(),
            P(),
            P(),
            P(("group", "dev"), None),
            P(("group", "dev")),
            P("group", "dev", None, None),
            P("group", "dev", None),
            P("group", "dev", None),
            P("group", "dev"),
            P("group", "dev", None, None, None),
        ),
        out_specs=(P(("group", "dev"), None), P(("group", "dev"), None), P(), P(), P()),
        check_vma=False,
    )
```

time: 1730 us -> 138 us (0.08)
  the two profiles are of different devices: /device:TPU:1 before, /device:TPU:67 now
where the time goes in v1:
time: 138 us; the launch traced here: 137 us
  Pallas kernels  120 us (87%)
  local copies, waits for them, and re-layouts  14.6 us (11%)
  other arithmetic  1.43 us (1%)
    pallas_call x1, Pallas kernels, return_call(): pl.pallas_call(functools.partial(return_kernel, groups, devs), out_shape=...  61.1 us
    pallas_call x1, Pallas kernels, gather_call(): pl.pallas_call(functools.partial(gather_kernel, groups, devs), out_shape=...  40.5 us
    pallas_call x1, Pallas kernels, layer_call(): pl.pallas_call(layer_kernel, out_shape=(jax.ShapeDtypeStruct((rows, width...  18.1 us
    unnamed x27, local copies, waits for them, and re-layouts  13.7 us

profile of v1, /device:TPU:67, one launch (start us, length us, event | category | flops | bytes accessed | tf_op | source)
XLA Modules:
  0.0 137.2 jit_solution(8821395975335248582)
XLA Ops:
  1.3 0.8 fusion
  2.1 0.1 broadcast_in_dim.12.hub_idx
  2.2 1.2 copy-done
  3.4 0.7 copy-done.8
  4.1 40.5 %halo_gather.1 = (bf16[32,128,256]{2,1,0:T(8,128)(2,1)S(1)}, bf16[2048,256]{1,0:T(8,128)(2,1)S(1)}) custom-call(bf16[2048,256]{1,0:T(8,128)(2,1)S(1)} %copy-done, s32[32,128]{1,0:T(8,128)S(1)} %bitcast.15, s32[16,128]{1,0:T(8,128)S(1)} %broadcast_in_dim.12.hub_idx), custom_call_target="tpu_custom_call" | custom-call | tf_op jit(solution)/shard_map/halo_gather/pallas_call | solution.py:196
  44.7 0.0 copy-start.4
  44.7 1.3 copy-done.4
  46.0 1.2 copy-done.1
  47.2 1.2 copy-done.5
  48.5 0.9 copy-done.6
  49.4 0.9 copy-done.7
  50.3 0.7 copy-done.10
  50.9 0.7 copy-done.11
  51.6 0.7 copy-done.12
  52.3 18.1 %layer.1 = (bf16[2048,256]{1,0:T(8,128)(2,1)}, bf16[32,128,256]{2,1,0:T(8,128)(2,1)}, bf16[8,2,128,256]{3,2,1,0:T(8,128)(2,1)S(1)}, f32[2048,256]{1,0:T(8,128)},...) custom-call(s32[128]{0:T(128)S(1)} %bitcast.18, s32[128]{0:T(128)S(1)} %bitcast.19, s32[1]{0:T(128)} %bitcast.13.count, ...), custom_call_target="tpu_custom_call" | custom-call | tf_op jit(solution)/shard_map/layer/pallas_call | solution.py:337
  70.4 0.0 copy-done.9
  70.4 0.0 copy-start.2
  70.4 1.6 %copy-done.2 = bf16[32,128,256]{2,1,0:T(8,128)(2,1)S(1)} copy-done((bf16[32,128,256]{2,1,0:T(8,128)(2,1)S(1)}, bf16[32,128,256]{2,1,0:T(8,128)(2,1)}, u32[]{:S(2)}) %copy-start.2) | copy-done | bytes 2097176
  72.0 1.6 %copy-done.3 = f32[2048,256]{1,0:T(8,128)S(1)} copy-done((f32[2048,256]{1,0:T(8,128)S(1)}, f32[2048,256]{1,0:T(8,128)}, u32[]{:S(2)}) %copy-start.3) | copy-done | bytes 2097176
  73.6 61.1 %halo_return.1 = (bf16[2048,256]{1,0:T(8,128)(2,1)S(1)}, bf16[32,16,256]{2,1,0:T(8,128)(2,1)S(1)}, f32[8,128]{1,0:T(8,128)S(1)}) custom-call(s32[32,128]{1,0:T(8,128)S(1)} %bitcast.16, s32[1,16]{1,0:T(1,128)S(1)} %get-tuple-element.29.hub_idx, bf16[32,128,256]{2,1,0:T(8,128)(2,1)S(1)} %copy-done.2, bf16[8,2,128,256]{3,2,1,0:T(8,128)(2,1)S(1)} %get-tuple-element.20.hub_back, ...), custom_call_target="tpu_custom_call" | custom-call | tf_op jit(solution)/shard_map/halo_return/pallas_call | solution.py:566
  134.7 0.6 multiply_bitcast_fusion
  135.3 0.1 convert_multiply_fusion
  135.4 0.8 fusion.1
  136.2 1.0 copy.18
  (11 shorter events, 0.0 us)
Async XLA Ops:
  2.2 1.2 copy-start
  3.4 0.7 copy-start.8
  44.7 1.3 copy-start.4
  46.0 1.2 copy-start.1
  47.2 1.2 copy-start.5
  48.5 0.9 copy-start.6
  49.4 0.9 copy-start.7
  50.3 0.7 copy-start.10
  50.9 0.7 copy-start.11
  51.6 0.7 copy-start.12
  52.3 18.2 %copy-start.9 = (s32[1,1,32,128]{3,2,1,0:T(8,128)S(1)}, s32[1,1,32,128]{3,2,1,0:T(8,128)}, u32[]{:S(2)}) copy-start(s32[1,1,32,128]{3,2,1,0:T(8,128)} %param.17) | copy-start | bytes 49156
  70.4 1.6 %copy-start.2 = (bf16[32,128,256]{2,1,0:T(8,128)(2,1)S(1)}, bf16[32,128,256]{2,1,0:T(8,128)(2,1)}, u32[]{:S(2)}) copy-start(bf16[32,128,256]{2,1,0:T(8,128)(2,1)} %get-tuple-element.19.halo_back) | copy-start | bytes 6291460
  72.0 1.6 %copy-start.3 = (f32[2048,256]{1,0:T(8,128)S(1)}, f32[2048,256]{1,0:T(8,128)}, u32[]{:S(2)}) copy-start(f32[2048,256]{1,0:T(8,128)} %get-tuple-element.21.own_back) | copy-start | bytes 6291460

commit v2 on v0

v2 whole, which is shorter than its diff:
```python
import functools
import math
import random

import jax
import jax.numpy as jnp
from jax import lax
from jax.experimental import pallas as pl
from jax.experimental.pallas import tpu as pltpu
from jax.sharding import PartitionSpec as P

MESH = pl.DeviceIdType.MESH
LANES = 128
BF16 = jnp.bfloat16
F32 = jnp.float32
I32 = jnp.int32
FIRST = (((0,), (0,)), ((), ()))
LAST = (((1,), (1,)), ((), ()))
MIB = 1 << 20
PART = 4
UNROLL = 8
ROWS_OF_PLAN = 8


def send_order(devs):
    ys = devs // 8
    every = [(y, x, c) for y in range(ys) for x in range(4) for c in range(2)][1:]
    draw = random.Random(5)
    draw.shuffle(every)
    other = [(-y % ys, -x % 4, c) for y, x, c in every]
    return every, other


class Place:
    def __init__(self, me, devs):
        self.me = me
        self.ys = devs // 8
        self.y = lax.div(me, 8)
        self.x = lax.rem(lax.div(me, 2), 4)
        self.core = lax.rem(me, 2)
        self.mate = me + 1 - 2 * self.core
        self.chip = lax.div(me, 2)
        self.plans = send_order(devs)

    def at(self, offset, sign):
        y, x, c = offset
        y, x = (y, x) if sign > 0 else (self.ys - y, 4 - x)
        return (
            lax.rem(self.y + y, self.ys) * 8
            + lax.rem(self.x + x, 4) * 2
            + lax.rem(self.core + c, 2)
        )

    def target(self, n):
        first, second = self.plans
        return jnp.where(self.core == 0, self.at(first[n], 1), self.at(second[n], 1))

    def source(self, n):
        first, second = self.plans
        sender = lax.rem(self.core + first[n][2], 2)
        return jnp.where(sender == 0, self.at(first[n], -1), self.at(second[n], -1))

    def across(self, n):
        chips = 4 * self.ys
        return lax.rem(self.chip + n, chips) * 2 + self.core


def column_of(row, size):
    return jnp.broadcast_to(row, (size, size)).T


def slot_plan(key, other, count, limit):
    size = key.shape[1]
    down = lax.broadcasted_iota(I32, (size, size), 0)
    along = lax.broadcasted_iota(I32, (size, size), 1)
    live = down < count
    keys = column_of(key, size)
    others = column_of(other, size)

    def total(mask, value=1):
        return jnp.sum(jnp.where(mask, value, 0), axis=0, keepdims=True)

    earlier = (keys == key) & (down < along)
    rank = total(earlier & live)
    odd = rank & 1
    ranks = column_of(rank, size)
    odds = ranks & 1
    heads = live & (odds == 0)
    pair = total(heads & ((keys < key) | earlier)) - odd
    pairs = column_of(pair, size)
    match = live & (pairs == along)
    left = match & (odds == 0)
    right = match & (odds == 1)
    has_right = total(right)
    place = along[:1]
    return [
        total(left, down),
        total(right, down) + (1 - has_right) * size,
        total(left, others),
        total(right, others),
        place * (1 - total(match & (ranks == 0))),
        total(heads & (keys <= along)) * jnp.minimum(total(live & (keys == along)), 1),
    ]


def layer_kernel(
    groups, devs,
    meta_hbm, lists_hbm, feat_hbm, vals_hbm, ws_hbm, wn_hbm, bias_hbm, cot_hbm,
    output, grad, wout, bias_out,
    meta, lists, vals, turned, ws, wn, bias, cot,
    table, runs, own_pre, aggb, dpre_ref, dagg, acc,
    halo_out, halo_in, hub_row, hub_pair, hub_send, hub_plane,
    pair_out, pair_in, z_out, z_in, row_out, row_in, wsend, w_in, wz_in, wfin,
    plan_v, plan_s,
    local, h_send, h_recv, m_sem, a_send, a_recv, z_send, z_recv, c_send, c_recv,
    g_send, g_recv, p_sem, s_send, s_recv, r_send, r_recv,
    w_send, w_recv, y_send, y_recv, f_send, f_recv,
):
    group = lax.axis_index("group")
    me = lax.axis_index("dev")
    here = Place(me, devs)
    core, mate, chip = here.core, here.mate, here.chip
    blocks, block, width = table.shape
    own_blocks = feat_hbm.shape[0]
    rows = own_blocks * block
    hub_start = own_blocks + devs
    capacity = vals_hbm.shape[0]
    share = hub_row.shape[0]
    chips = devs // 2
    messages = devs - 1

    def fetch(src, dst, which):
        copy = pltpu.make_async_copy(src, dst, local.at[which])
        copy.start()
        return copy

    early = [
        fetch(feat_hbm, table.at[pl.ds(0, own_blocks)], 0),
        fetch(lists_hbm, lists, 1),
        fetch(meta_hbm, meta, 2),
    ]

    def to_plane(src, dst, send, recv, peer):
        return pltpu.make_async_remote_copy(
            src_ref=src, dst_ref=dst, send_sem=send, recv_sem=recv,
            device_id={"dev": peer}, device_id_type=MESH,
        )

    def to_column(src, dst, send, recv, peer):
        return pltpu.make_async_remote_copy(
            src_ref=src, dst_ref=dst, send_sem=send, recv_sem=recv,
            device_id={"group": peer}, device_id_type=MESH,
        )

    def above(step):
        return lax.rem(group + step, groups)

    barrier = pltpu.get_barrier_semaphore()
    for n in range(messages):
        pl.semaphore_signal(
            barrier, inc=1, device_id={"dev": here.target(n)}, device_id_type=MESH
        )
    for step in range(1, groups):
        pl.semaphore_signal(
            barrier, inc=1, device_id={"group": above(step)}, device_id_type=MESH
        )
    late = [
        fetch(vals_hbm, vals.at[pl.ds(0, capacity)], 3),
        fetch(ws_hbm, ws, 4),
        fetch(wn_hbm, wn, 5),
        fetch(bias_hbm, bias, 6),
        fetch(cot_hbm, cot, 7),
    ]
    for copy in early:
        copy.wait()

    lane = lax.broadcasted_iota(I32, (block, LANES), 1)
    owned = pl.ds(0, own_blocks)

    def onehot(column, ids):
        return jnp.concatenate(
            [
                jnp.where(column == ids + LANES * r, 1.0, 0.0).astype(BF16)
                for r in range(rows // LANES)
            ],
            axis=1,
        )

    def pick(matrix):
        return jnp.dot(matrix, table[owned].reshape(rows, width), preferred_element_type=F32)

    hubs_row = meta[pl.ds(3, 1), :]
    picked = pick(onehot(column_of(hubs_row, block)[: 2 * share], lane[: 2 * share]))[:share]
    hub_row[...] = picked
    hub_pair[core] = picked

    def fill(low, high):
        parts = [
            onehot(column_of(lists[pl.ds(here.target(n), 1), :], block), lane)
            for n in range(low, high)
        ]
        got = pick(jnp.concatenate(parts, axis=0)).astype(BF16)
        halo_out[pl.ds(low, high - low)] = got.reshape(high - low, block, width)

    def halo_copy(n):
        return to_plane(
            halo_out.at[n], table.at[own_blocks + me], h_send.at[n], h_recv.at[me], here.target(n)
        )

    def from_plane(dst, send, recv, peer):
        return to_plane(dst, dst, send, recv, peer)

    spans = [(low, min(low + PART, messages)) for low in range(0, messages, PART)]

    def ship(span):
        for n in range(*span):
            halo_copy(n).start()

    hub_mate = to_plane(hub_row, hub_pair.at[core], m_sem.at[0], m_sem.at[1], mate)

    def hub_spread(n):
        return to_plane(
            hub_send, hub_plane.at[chip], a_send.at[n], a_recv.at[chip], here.across(n)
        )

    def hub_block(owner, side):
        return table.at[hub_start + owner * 2 + side]

    half_chips = chips // 2

    def hub_up(step):
        return to_column(
            hub_plane.at[pl.ds(core * half_chips, half_chips)],
            hub_in_table(group, core),
            z_send.at[step], z_recv.at[group], above(step),
        )

    def hub_in_table(owner, side):
        return hub_table.at[pl.ds((owner * 2 + side) * half_chips, half_chips)]

    hub_table = table.at[pl.ds(hub_start, blocks - hub_start)].reshape(
        (blocks - hub_start) * half_chips, 2 * share, width
    )

    fill(*spans[0])
    pl.semaphore_wait(barrier, devs + groups - 2)
    hub_mate.start()
    ship(spans[0])
    fill(*spans[1])
    ship(spans[1])

    hub_mate.wait_recv()
    both = hub_pair[...].reshape(2 * share, width).astype(BF16)
    hub_send[...] = both
    hub_plane[chip] = both
    for n in range(1, chips):
        hub_spread(n).start()

    for span in spans[2:4]:
        fill(*span)
        ship(span)

    for n in range(1, chips):
        source = lax.div(here.across(n), 2)
        from_plane(hub_plane.at[source], a_send.at[n], a_recv.at[source], mate).wait_recv()
    for step in range(1, groups):
        hub_up(step).start()
    hub_table[pl.ds(group * chips, chips)] = hub_plane[...]

    for span in spans[4:]:
        fill(*span)
        ship(span)

    count = meta[pl.ds(2, 1), :]
    src = meta[pl.ds(0, 1), :]
    tgt = meta[pl.ds(1, 1), :]
    ahead = slot_plan(tgt, src, count, own_blocks)
    back = slot_plan(src, tgt, count, blocks)
    for at, row in enumerate(ahead):
        plan_v[pl.ds(at, 1), :] = row
    for at, row in enumerate(back):
        plan_v[pl.ds(ROWS_OF_PLAN + at, 1), :] = row
    plan_copy = fetch(plan_v, plan_s, 8)
    table[own_blocks + me] = jnp.zeros((block, width), BF16)
    vals[capacity] = jnp.zeros((block, block), BF16)
    turned[capacity] = jnp.zeros((block, block), BF16)
    runs[0] = jnp.zeros((block, width), F32)
    for copy in late:
        copy.wait()

    def turn(step, _):
        for u in range(UNROLL):
            k = step * UNROLL + u
            turned[k] = vals[k].T
        return _

    lax.fori_loop(0, capacity // UNROLL, turn, 0)

    def span_of(t):
        return pl.ds(pl.multiple_of(t * 2 * block, 2 * block), 2 * block)

    def own_part(t, _):
        own = table[pl.ds(t * 2, 2)].reshape(2 * block, width)
        own_pre[span_of(t), :] = (
            jnp.dot(own, ws[...], preferred_element_type=F32) + bias[...]
        )
        return _

    lax.fori_loop(0, own_blocks // 2, own_part, 0)
    plan_copy.wait()

    def pass_on(step):
        owner = lax.rem(group + groups - step, groups)
        part = hub_in_table(owner, core)
        to_column(part, part, z_send.at[step], z_recv.at[owner], owner).wait_recv()
        to_plane(part, part, c_send.at[owner], c_recv.at[owner], mate).start()

    for step in range(1, groups):
        pass_on(step)

    for step in range(1, groups):
        owner = lax.rem(group + groups - step, groups)
        sent, got = hub_in_table(owner, core), hub_in_table(owner, 1 - core)
        to_plane(sent, sent, c_send.at[owner], c_recv.at[owner], mate).wait_send()
        to_plane(got, got, c_send.at[owner], c_recv.at[owner], mate).wait_recv()
    for n in range(messages):
        source = here.source(n)
        from_plane(
            table.at[own_blocks + source], h_send.at[n], h_recv.at[source], source
        ).wait_recv()

    def forward(step, _):
        for u in range(UNROLL):
            p = step * UNROLL + u
            left = jnp.concatenate([vals[plan_s[0, p]], vals[plan_s[1, p]]], axis=1)
            right = jnp.concatenate([table[plan_s[2, p]], table[plan_s[3, p]]], axis=0)
            runs[p + 1] = runs[plan_s[4, p]] + jnp.dot(left, right, preferred_element_type=F32)
        return _

    lax.fori_loop(0, pl.cdiv(capacity + own_blocks, 2 * UNROLL), forward, 0)

    def dense(t, _):
        at = span_of(t)
        near = jnp.concatenate(
            [runs[plan_s[5, t * 2]], runs[plan_s[5, t * 2 + 1]]], axis=0
        ).astype(BF16)
        aggb[at, :] = near
        pre = own_pre[at, :] + jnp.dot(near, wn[...], preferred_element_type=F32)
        sigmoid = jax.nn.sigmoid(pre)
        output[at, :] = (pre * sigmoid).astype(BF16)
        slope = sigmoid * (1.0 + pre * (1.0 - sigmoid))
        dpre = (cot[at, :].astype(F32) * slope).astype(BF16)
        dpre_ref[at, :] = dpre
        dagg[pl.ds(t * 2, 2)] = (
            lax.dot_general(dpre, wn[...], LAST, preferred_element_type=F32)
            .astype(BF16)
            .reshape(2, block, width)
        )
        return _

    lax.fori_loop(0, own_blocks // 2, dense, 0)

    part_rows = wsend.shape[1]
    dpre_all = dpre_ref[...]
    gself = lax.dot_general(
        table[owned].reshape(rows, width), dpre_all, FIRST, preferred_element_type=F32
    )
    gneigh = lax.dot_general(aggb[...], dpre_all, FIRST, preferred_element_type=F32)
    gbias = jnp.sum(dpre_all.astype(F32), axis=0, keepdims=True)
    half = devs // 2
    wide = pl.ds(0, width)
    wsend[pl.ds(0, half), :, wide] = gself.astype(BF16).reshape(half, part_rows, width)
    wsend[pl.ds(half, half), :, wide] = gneigh.astype(BF16).reshape(half, part_rows, width)
    line = lax.broadcasted_iota(I32, (part_rows, LANES), 0)
    sums = jnp.where(line == 0, gbias[:, :LANES], jnp.where(line == 1, gbias[:, LANES:], 0.0))
    wsend[:, :, pl.ds(width, LANES)] = jnp.broadcast_to(
        sums.astype(BF16)[None], (devs, part_rows, LANES)
    )

    def w_copy(n):
        peer = here.target(n)
        return to_plane(wsend.at[peer], w_in.at[me], w_send.at[n], w_recv.at[me], peer)

    for n in range(messages):
        w_copy(n).start()
    w_in[me] = wsend[me]
    for n in range(messages):
        halo_copy(n).wait_send()

    def backward(step, _):
        for u in range(UNROLL):
            p = step * UNROLL + u
            left = jnp.concatenate(
                [turned[plan_s[ROWS_OF_PLAN, p]], turned[plan_s[ROWS_OF_PLAN + 1, p]]], axis=1
            )
            right = jnp.concatenate(
                [dagg[plan_s[ROWS_OF_PLAN + 2, p]], dagg[plan_s[ROWS_OF_PLAN + 3, p]]], axis=0
            )
            runs[p + 1] = runs[plan_s[ROWS_OF_PLAN + 4, p]] + jnp.dot(
                left, right, preferred_element_type=F32
            )
        return _

    lax.fori_loop(0, pl.cdiv(capacity + blocks, 2 * UNROLL), backward, 0)

    def dtable(b):
        return runs[plan_s[ROWS_OF_PLAN + 5, b]]

    def back_copy(n):
        return to_plane(halo_out.at[n], halo_in.at[me], g_send.at[n], g_recv.at[me], here.target(n))

    for n in range(messages):
        halo_out[n] = dtable(own_blocks + here.target(n)).astype(BF16)
        back_copy(n).start()
    for k in range(groups):
        pair_out[k] = dtable(hub_start + 2 * k + 1 - core).astype(BF16)
    pair = to_plane(pair_out, pair_in, p_sem.at[0], p_sem.at[1], mate)
    pair.start()

    for n in range(messages):
        source = here.source(n)
        from_plane(w_in.at[source], w_send.at[n], w_recv.at[source], source).wait_recv()
    wz_in[group] = jnp.sum(w_in[...].astype(F32), axis=0).astype(BF16)

    def y_copy(step):
        return to_column(
            wz_in.at[group], wz_in.at[group], y_send.at[step], y_recv.at[group], above(step)
        )

    for step in range(1, groups):
        y_copy(step).start()

    pair.wait_recv()
    for k in range(groups):
        z_out[k] = (dtable(hub_start + 2 * k + core) + pair_in[k].astype(F32)).astype(BF16)

    def s_copy(step):
        return to_column(
            z_out.at[above(step)], z_in.at[group], s_send.at[step], s_recv.at[group], above(step)
        )

    for step in range(1, groups):
        s_copy(step).start()
    z_in[group] = z_out[group]

    def begin(t, _):
        at = span_of(t)
        own = jnp.concatenate([dtable(t * 2), dtable(t * 2 + 1)], axis=0)
        acc[at, :] = own + lax.dot_general(
            dpre_ref[at, :], ws[...], LAST, preferred_element_type=F32
        )
        return _

    lax.fori_loop(0, own_blocks // 2, begin, 0)

    for step in range(1, groups):
        peer = above(step)
        to_column(
            wz_in.at[peer], wz_in.at[peer], y_send.at[step], y_recv.at[peer], peer
        ).wait_recv()
    total = jnp.sum(wz_in[...].astype(F32), axis=0)
    wfin[me] = total[:, :width].astype(BF16)
    bias_out[...] = total[:8, width:]

    def f_copy(n):
        return to_plane(
            wfin.at[me], wfin.at[me], f_send.at[n], f_recv.at[me], here.target(n)
        )

    for n in range(messages):
        f_copy(n).start()

    def scatter(span):
        ids, got = [], []
        for n in range(*span):
            source = here.source(n)
            from_plane(halo_in.at[source], g_send.at[n], g_recv.at[source], source).wait_recv()
            ids.append(lists[pl.ds(source, 1), :])
            got.append(halo_in[source])
        ids = jnp.concatenate(ids, axis=1)
        got = jnp.concatenate(got, axis=0)

        def add(t, _):
            node = lax.broadcasted_iota(I32, (2 * block, ids.shape[1]), 0) + t * (2 * block)
            chosen = jnp.where(node == ids, 1.0, 0.0).astype(BF16)
            acc[span_of(t), :] += jnp.dot(chosen, got, preferred_element_type=F32)
            return _

        lax.fori_loop(0, own_blocks // 2, add, 0)

    for span in spans[:3]:
        scatter(span)

    for step in range(1, groups):
        peer = above(step)
        to_column(
            z_out.at[peer], z_in.at[peer], s_send.at[step], s_recv.at[peer], peer
        ).wait_recv()
    row_out[...] = jnp.sum(z_in[...].astype(F32), axis=0).reshape(row_out.shape)

    def row_copy(k):
        return to_plane(
            row_out.at[k], row_in.at[chip], r_send.at[k], r_recv.at[chip], core * chips + k
        )

    for k in range(chips):
        @pl.when(core * chips + k != me)
        def _():
            row_copy(k).start()

        @pl.when(core * chips + k == me)
        def _():
            row_in[chip] = row_out[k]

    for span in spans[3:]:
        scatter(span)

    side = lax.div(me, chips)
    for k in range(chips):
        sender = k * 2 + side

        @pl.when(sender != me)
        def _():
            to_plane(row_out.at[k], row_in.at[k], r_send.at[k], r_recv.at[k], sender).wait_recv()

    hub_sum = jnp.sum(row_in[...], axis=0)
    top = hub_sum.astype(BF16).astype(F32)
    both = jnp.concatenate([top, hub_sum - top], axis=0).astype(BF16)
    hub_ids = meta[pl.ds(3, 1), :][:, : 2 * share]

    def finish(t, _):
        at = span_of(t)
        node = lax.broadcasted_iota(I32, (2 * block, 2 * share), 0) + t * (2 * block)
        chosen = jnp.where(node == hub_ids, 1.0, 0.0).astype(BF16)
        grad[at, :] = (
            acc[at, :] + jnp.dot(chosen, both, preferred_element_type=F32)
        ).astype(BF16)
        return _

    lax.fori_loop(0, own_blocks // 2, finish, 0)

    for n in range(messages):
        source = here.source(n)
        from_plane(wfin.at[source], f_send.at[n], f_recv.at[source], source).wait_recv()
    wout[...] = wfin[...]

    hub_mate.wait_send()
    pair.wait_send()
    for n in range(1, chips):
        hub_spread(n).wait_send()
    for step in range(1, groups):
        hub_up(step).wait_send()
        y_copy(step).wait_send()
        s_copy(step).wait_send()
    for n in range(messages):
        w_copy(n).wait_send()
        back_copy(n).wait_send()
        f_copy(n).wait_send()
    for k in range(chips):
        @pl.when(core * chips + k != me)
        def _():
            row_copy(k).wait_send()


def layer_call(meta, lists, features, values, ws, wn, bias, cot, groups, devs, share):
    own_blocks, block, width = features.shape
    rows = own_blocks * block
    capacity = values.shape[0]
    hubs = groups * devs * share
    blocks = own_blocks + devs + hubs // block
    chips = devs // 2
    part_rows = 2 * width // devs
    most = UNROLL * pl.cdiv(capacity + blocks, 2 * UNROLL)
    dma = pltpu.SemaphoreType.DMA
    vm = pltpu.VMEM
    anywhere = pl.BlockSpec(memory_space=pl.ANY)
    vmem = pl.BlockSpec(memory_space=pltpu.VMEM)
    return pl.pallas_call(
        functools.partial(layer_kernel, groups, devs),
        out_shape=(
            jax.ShapeDtypeStruct((rows, width), BF16),
            jax.ShapeDtypeStruct((rows, width), BF16),
            jax.ShapeDtypeStruct((devs, part_rows, width), BF16),
            jax.ShapeDtypeStruct((8, LANES), F32),
        ),
        in_specs=[anywhere] * 8,
        out_specs=[vmem] * 4,
        scratch_shapes=[
            vm(meta.shape, I32), vm(lists.shape, I32),
            vm((capacity + 1, block, block), BF16), vm((capacity + 1, block, block), BF16),
            vm((width, width), BF16), vm((width, width), BF16), vm((1, width), F32),
            vm((rows, width), BF16),
            vm((blocks, block, width), BF16), vm((most + 1, block, width), F32),
            vm((rows, width), F32), vm((rows, width), BF16), vm((rows, width), BF16),
            vm((own_blocks, block, width), BF16), vm((rows, width), F32),
            vm((devs, block, width), BF16), vm((devs, block, width), BF16),
            vm((share, width), F32), vm((2, share, width), F32),
            vm((2 * share, width), BF16), vm((chips, 2 * share, width), BF16),
            vm((groups, block, width), BF16), vm((groups, block, width), BF16),
            vm((groups, block, width), BF16), vm((groups, block, width), BF16),
            vm((chips, share, width), F32), vm((chips, share, width), F32),
            vm((devs, part_rows, width + LANES), BF16), vm((devs, part_rows, width + LANES), BF16),
            vm((groups, part_rows, width + LANES), BF16), vm((devs, part_rows, width), BF16),
            vm((2 * ROWS_OF_PLAN, LANES), I32), pltpu.SMEM((2 * ROWS_OF_PLAN, LANES), I32),
            dma((9,)), dma((devs,)), dma((devs,)), dma((2,)), dma((chips,)), dma((chips,)),
            dma((groups,)), dma((groups,)), dma((groups,)), dma((groups,)),
            dma((devs,)), dma((devs,)), dma((2,)), dma((groups,)), dma((groups,)),
            dma((chips,)), dma((chips,)),
            dma((devs,)), dma((devs,)), dma((groups,)), dma((groups,)), dma((devs,)), dma((devs,)),
        ],
        compiler_params=pltpu.CompilerParams(
            collective_id=0, has_side_effects=True, vmem_limit_bytes=56 * MIB
        ),
        name="layer",
    )(meta, lists, features, values, ws, wn, bias, cot)


def shards(groups, devs, features, weight_self, weight_neigh, bias, cotangent, hub_rows,
           halo_send, block_src, block_tgt, block_count, block_vals):
    rows, width = features.shape
    scale = 1.0 / math.sqrt(rows * groups * devs)
    share = hub_rows.shape[0]
    block = block_vals.shape[-1]
    unused = jnp.full((LANES - 2 * share,), -1, I32)
    meta = jnp.stack(
        [
            block_src[0, 0],
            block_tgt[0, 0],
            jnp.broadcast_to(block_count[0, 0], (LANES,)),
            jnp.concatenate([hub_rows, hub_rows, unused]),
        ]
    )
    meta = jnp.concatenate([meta, jnp.zeros((4, LANES), I32)])
    output, grad, wout, bias_out = layer_call(
        meta, halo_send[0, 0], features.reshape(-1, block, width), block_vals[0, 0],
        weight_self, weight_neigh, bias[None], cotangent, groups, devs, share,
    )
    wgrad = wout.reshape(2, width, width).astype(F32) * scale
    return output, grad, wgrad[0], wgrad[1], bias_out[:2].reshape(width) * scale


def solution(mesh):
    groups, devs = mesh.shape["group"], mesh.shape["dev"]
    return jax.shard_map(
        functools.partial(shards, groups, devs),
        mesh=mesh,
        in_specs=(
            P(("group", "dev"), None),
            P(),
            P(),
            P(),
            P(("group", "dev"), None),
            P(("group", "dev")),
            P("group", "dev", None, None),
            P("group", "dev", None),
            P("group", "dev", None),
            P("group", "dev"),
            P("group", "dev", None, None, None),
        ),
        out_specs=(P(("group", "dev"), None), P(("group", "dev"), None), P(), P(), P()),
        check_vma=False,
    )
```

time: 1730 us -> 97.1 us (0.06)
  waiting for transfers between devices: 1420 us -> 0 us
  other arithmetic: 96.5 us -> 3.13 us
  blocking collectives: 91.9 us -> 0 us
  Pallas kernels: 0 us -> 87.1 us
  local copies, waits for them, and re-layouts: 51.9 us -> 5.35 us
  matrix products: 37.5 us -> 0 us
    reduce_scatter x1 -> x0, waiting for transfers between devices: 1240 us -> none  [shards(): lax.psum_scatter(hub_part, ('group', 'dev'), scatter_dimension=0, tiled=T...]
    psum x1 -> x0, waiting for transfers between devices: 98.8 us -> none  [shards(): lax.psum((grad_self, grad_neigh, grad_bias), ('group', 'dev'))]
    psum x1 -> x0, blocking collectives: 91.9 us -> none  [shards(): lax.psum((grad_self, grad_neigh, grad_bias), ('group', 'dev'))]
    scatter-add x4 -> x0, other arithmetic: 90.1 us -> none  [the longest x1 38.8 us: shards(): dtable = jax.ops.segment_sum(back, sources, num_segments=src_blocks)]
    pallas_call x0 -> x1, Pallas kernels: none -> 87.1 us  [layer_call(): pl.pallas_call(functools.partial(layer_kernel, groups, devs), out_shape=(...]
    all_gather x1 -> x0, waiting for transfers between devices: 54.4 us -> none  [shards(): hubs = lax.all_gather(mine, ('group', 'dev'), axis=0, tiled=True)]
    dot_general x8 -> x0, matrix products: 37.5 us -> none  [the longest x1 13.9 us: shards(): jnp.einsum('kji,kjf->kif', masked, dagg_tiles, preferred_element_type=jnp...]
    gather x4 -> x0, local copies, waits for them, and re-layouts: 34.8 us -> none  [the longest x1 16.9 us: shards(): outgoing = padded[send_lists]]
  transfers between devices with their start and end apart: 5 -> 0, of which waited for: 4 -> 0; matrix products, arithmetic and copies ran while one was open for 6% -> 0% of each run, Pallas kernels for 0% -> 0%
where the time goes in v2:
time: 97.1 us; the launch traced here: 96.9 us
  Pallas kernels  87.1 us (90%)
  local copies, waits for them, and re-layouts  5.35 us (6%)
  other arithmetic  3.13 us (3%)
  between operations  1.32 us (1%)
    pallas_call x1, Pallas kernels, layer_call(): pl.pallas_call(functools.partial(layer_kernel, groups, devs), out_shape=(...  87.1 us
    unnamed x4, local copies, waits for them, and re-layouts  3.24 us

profile of v2, /device:TPU:1, one launch (start us, length us, event | category | flops | bytes accessed | tf_op | source)
XLA Modules:
  0.0 96.9 jit_solution(7671770098211620209)
XLA Ops:
  1.3 0.8 add_bitcast_fusion
  2.1 1.3 %concatenate.7.meta_hbm = s32[8,128]{1,0:T(8,128)} concatenate(s32[1,128]{1,0:T(1,128)} %bitcast.20, s32[1,128]{1,0:T(1,128)} %bitcast.21, s32[1,128]{1,0:T(1,128)S(1)} %stack_broadcast_in_dim.3, s32[1,128]{1,0:T(1,128)S(1)} %add_bitcast_fusion, s32[4,128]{1,0:T(4,128)S(1)} %broadcast_in_dim.10), dimensions={0} | concatenate | bytes 8192 | tf_op jit(solution)/shard_map/concatenate | solution.py:633
  3.4 87.1 %layer.1 = (bf16[2048,256]{1,0:T(8,128)(2,1)}, bf16[2048,256]{1,0:T(8,128)(2,1)}, bf16[32,16,256]{2,1,0:T(8,128)(2,1)}, f32[8,128]{1,0:T(8,128)}) custom-call(s32[8,128]{1,0:T(8,128)} %concatenate.7.meta_hbm, s32[32,128]{1,0:T(8,128)} %bitcast.18, bf16[16,128,256]{2,1,0:T(8,128)(2,1)} %bitcast.15, bf16[128,128,128]{2,1,0:T(8,128)(2,1)} %bitcast.14, ...), custom_call_target="tpu_custom_call" | custom-call | tf_op jit(solution)/shard_map/layer/pallas_call | solution.py:578
  90.5 0.0 copy-start
  90.5 1.1 %convert_multiply_fusion = f32[32,16,256]{2,1,0:T(8,128)S(1)} fusion(bf16[32,16,256]{2,1,0:T(8,128)(2,1)} %get-tuple-element.11), kind=kLoop, calls=%fused_computation | loop fusion | flops 262144 | bytes 786432 | tf_op jit(solution)/shard_map/mul | solution.py:638
  91.6 0.8 fusion
  92.4 1.2 %multiply_bitcast_fusion = f32[256]{0:T(256)} fusion(f32[8,128]{1,0:T(8,128)} %get-tuple-element.12), kind=kLoop, calls=%fused_computation.1 | loop fusion | flops 256 | bytes 2048 | tf_op jit(solution)/shard_map/mul | solution.py:639
  93.6 2.3 %copy.19 = bf16[2048,256]{1,0:T(8,128)(2,1)} copy(bf16[2048,256]{1,0:T(8,128)(2,1)} %get-tuple-element.20) | data formatting | bytes 2097152
  95.9 0.0 copy-done
  95.9 1.0 %copy.20 = bf16[2048,256]{1,0:T(8,128)(2,1)} copy(bf16[2048,256]{1,0:T(8,128)(2,1)S(1)} %copy-done) | data formatting | bytes 2097152
  (3 shorter events, 0.0 us)
Async XLA Ops:
  90.5 5.4 %copy-start = (bf16[2048,256]{1,0:T(8,128)(2,1)S(1)}, bf16[2048,256]{1,0:T(8,128)(2,1)}, u32[]{:S(2)}) copy-start(bf16[2048,256]{1,0:T(8,128)(2,1)} %get-tuple-element.21) | copy-start | bytes 3145732

commit v3 on v2

--- a/solution.py
+++ b/solution.py
@@ -20,6 +20,8 @@
 PART = 4
 UNROLL = 8
 ROWS_OF_PLAN = 8
+TILE = 512
+LOW = 256
 
 
 def send_order(devs):
@@ -105,10 +107,10 @@
 
 def layer_kernel(
     groups, devs,
-    meta_hbm, lists_hbm, feat_hbm, vals_hbm, ws_hbm, wn_hbm, bias_hbm, cot_hbm,
-    output, grad, wout, bias_out,
-    meta, lists, vals, turned, ws, wn, bias, cot,
-    table, runs, own_pre, aggb, dpre_ref, dagg, acc,
+    hub_rows, counts, src_hbm, tgt_hbm, lists_hbm, feat_hbm, vals_hbm, ws_hbm, wn_hbm, bias_hbm, cot_hbm,
+    output_hbm, grad_hbm, wout, bias_out,
+    src_v, tgt_v, output, grad, bias_sum, wide, lists, vals, turned, ws, wn, bias, cot,
+    table, runs, own_pre, dpre_ref, dagg, acc,
     halo_out, halo_in, hub_row, hub_pair, hub_send, hub_plane,
     pair_out, pair_in, z_out, z_in, row_out, row_in, wsend, w_in, wz_in, wfin,
     plan_v, plan_s,
@@ -137,7 +139,6 @@
     early = [
         fetch(feat_hbm, table.at[pl.ds(0, own_blocks)], 0),
         fetch(lists_hbm, lists, 1),
-        fetch(meta_hbm, meta, 2),
     ]
 
     def to_plane(src, dst, send, recv, peer):
@@ -170,6 +171,8 @@
         fetch(wn_hbm, wn, 5),
         fetch(bias_hbm, bias, 6),
         fetch(cot_hbm, cot, 7),
+        fetch(src_hbm, src_v, 2),
+        fetch(tgt_hbm, tgt_v, 9),
     ]
     for copy in early:
         copy.wait()
@@ -177,26 +180,35 @@
     lane = lax.broadcasted_iota(I32, (block, LANES), 1)
     owned = pl.ds(0, own_blocks)
 
-    def onehot(column, ids):
-        return jnp.concatenate(
+    def onehot(column):
+        low = column & (LOW - 1)
+        high = lax.shift_right_logical(column, 8).astype(F32).astype(BF16)
+        high = jnp.concatenate([high] * (LOW // LANES), axis=1)
+        ones = jnp.concatenate(
             [
-                jnp.where(column == ids + LANES * r, 1.0, 0.0).astype(BF16)
-                for r in range(rows // LANES)
+                jnp.where(low == lane[: column.shape[0]] + LANES * r, 1.0, 0.0)
+                for r in range(LOW // LANES)
             ],
             axis=1,
+        ).astype(BF16)
+        none = jnp.zeros_like(ones)
+        return jnp.concatenate(
+            [jnp.where(high == float(t), ones, none) for t in range(rows // LOW)], axis=1
         )
 
     def pick(matrix):
         return jnp.dot(matrix, table[owned].reshape(rows, width), preferred_element_type=F32)
 
-    hubs_row = meta[pl.ds(3, 1), :]
-    picked = pick(onehot(column_of(hubs_row, block)[: 2 * share], lane[: 2 * share]))[:share]
+    hub_ids = jnp.full((1, block), rows, I32)
+    for k in range(share):
+        hub_ids = jnp.where((lane[:1] == k) | (lane[:1] == k + share), hub_rows[k], hub_ids)
+    picked = pick(onehot(column_of(hub_ids, block)[: 2 * share]))[:share]
     hub_row[...] = picked
     hub_pair[core] = picked
 
     def fill(low, high):
         parts = [
-            onehot(column_of(lists[pl.ds(here.target(n), 1), :], block), lane)
+            onehot(column_of(lists[pl.ds(here.target(n), 1), :], block))
             for n in range(low, high)
         ]
         got = pick(jnp.concatenate(parts, axis=0)).astype(BF16)
@@ -247,7 +259,6 @@
     hub_mate.start()
     ship(spans[0])
     fill(*spans[1])
-    ship(spans[1])
 
     hub_mate.wait_recv()
     both = hub_pair[...].reshape(2 * share, width).astype(BF16)
@@ -255,8 +266,9 @@
     hub_plane[chip] = both
     for n in range(1, chips):
         hub_spread(n).start()
-
-    for span in spans[2:4]:
+    ship(spans[1])
+
+    for span in spans[2:]:
         fill(*span)
         ship(span)
 
@@ -267,13 +279,11 @@
         hub_up(step).start()
     hub_table[pl.ds(group * chips, chips)] = hub_plane[...]
 
-    for span in spans[4:]:
-        fill(*span)
-        ship(span)
-
-    count = meta[pl.ds(2, 1), :]
-    src = meta[pl.ds(0, 1), :]
-    tgt = meta[pl.ds(1, 1), :]
+    for copy in late:
+        copy.wait()
+    count = counts[0, 0]
+    src = src_v[...]
+    tgt = tgt_v[...]
     ahead = slot_plan(tgt, src, count, own_blocks)
     back = slot_plan(src, tgt, count, blocks)
     for at, row in enumerate(ahead):
@@ -285,8 +295,7 @@
     vals[capacity] = jnp.zeros((block, block), BF16)
     turned[capacity] = jnp.zeros((block, block), BF16)
     runs[0] = jnp.zeros((block, width), F32)
-    for copy in late:
-        copy.wait()
+    wide[pl.ds(2 * width, 16), :] = jnp.ones((16, rows), BF16)
 
     def turn(step, _):
         for u in range(UNROLL):
@@ -304,6 +313,7 @@
         own_pre[span_of(t), :] = (
             jnp.dot(own, ws[...], preferred_element_type=F32) + bias[...]
         )
+        wide[pl.ds(0, width), span_of(t)] = own.T
         return _
 
     lax.fori_loop(0, own_blocks // 2, own_part, 0)
@@ -339,16 +349,17 @@
 
     lax.fori_loop(0, pl.cdiv(capacity + own_blocks, 2 * UNROLL), forward, 0)
 
-    def dense(t, _):
+    def dense_part(t):
         at = span_of(t)
         near = jnp.concatenate(
             [runs[plan_s[5, t * 2]], runs[plan_s[5, t * 2 + 1]]], axis=0
         ).astype(BF16)
-        aggb[at, :] = near
+        wide[pl.ds(width, width), at] = near.T
         pre = own_pre[at, :] + jnp.dot(near, wn[...], preferred_element_type=F32)
-        sigmoid = jax.nn.sigmoid(pre)
-        output[at, :] = (pre * sigmoid).astype(BF16)
-        slope = sigmoid * (1.0 + pre * (1.0 - sigmoid))
+        sigmoid = 0.5 * jnp.tanh(0.5 * pre) + 0.5
+        result = pre * sigmoid
+        output[at, :] = result.astype(BF16)
+        slope = sigmoid + result * (1.0 - sigmoid)
         dpre = (cot[at, :].astype(F32) * slope).astype(BF16)
         dpre_ref[at, :] = dpre
         dagg[pl.ds(t * 2, 2)] = (
@@ -356,21 +367,21 @@
             .astype(BF16)
             .reshape(2, block, width)
         )
+
+    def dense(step, _):
+        dense_part(step * 2)
+        dense_part(step * 2 + 1)
         return _
 
-    lax.fori_loop(0, own_blocks // 2, dense, 0)
+    lax.fori_loop(0, own_blocks // 4, dense, 0)
+    output_copy = fetch(output, output_hbm, 10)
 
     part_rows = wsend.shape[1]
-    dpre_all = dpre_ref[...]
-    gself = lax.dot_general(
-        table[owned].reshape(rows, width), dpre_all, FIRST, preferred_element_type=F32
+    sums = jnp.dot(wide[...], dpre_ref[...], preferred_element_type=F32)
+    wsend[:, :, pl.ds(0, width)] = (
+        sums[: 2 * width].astype(BF16).reshape(devs, part_rows, width)
     )
-    gneigh = lax.dot_general(aggb[...], dpre_all, FIRST, preferred_element_type=F32)
-    gbias = jnp.sum(dpre_all.astype(F32), axis=0, keepdims=True)
-    half = devs // 2
-    wide = pl.ds(0, width)
-    wsend[pl.ds(0, half), :, wide] = gself.astype(BF16).reshape(half, part_rows, width)
-    wsend[pl.ds(half, half), :, wide] = gneigh.astype(BF16).reshape(half, part_rows, width)
+    gbias = sums[2 * width : 2 * width + 1]
     line = lax.broadcasted_iota(I32, (part_rows, LANES), 0)
     sums = jnp.where(line == 0, gbias[:, :LANES], jnp.where(line == 1, gbias[:, LANES:], 0.0))
     wsend[:, :, pl.ds(width, LANES)] = jnp.broadcast_to(
@@ -460,7 +471,8 @@
         ).wait_recv()
     total = jnp.sum(wz_in[...].astype(F32), axis=0)
     wfin[me] = total[:, :width].astype(BF16)
-    bias_out[...] = total[:8, width:]
+    bias_sum[...] = total[:8, width:]
+    bias_copy = fetch(bias_sum, bias_out, 11)
 
     def f_copy(n):
         return to_plane(
@@ -479,16 +491,17 @@
             got.append(halo_in[source])
         ids = jnp.concatenate(ids, axis=1)
         got = jnp.concatenate(got, axis=0)
-
-        def add(t, _):
-            node = lax.broadcasted_iota(I32, (2 * block, ids.shape[1]), 0) + t * (2 * block)
-            chosen = jnp.where(node == ids, 1.0, 0.0).astype(BF16)
-            acc[span_of(t), :] += jnp.dot(chosen, got, preferred_element_type=F32)
-            return _
-
-        lax.fori_loop(0, own_blocks // 2, add, 0)
-
-    for span in spans[:3]:
+        low = ids & (TILE - 1)
+        node = lax.broadcasted_iota(I32, (TILE, ids.shape[1]), 0)
+        ones = jnp.where(node == low, 1.0, 0.0).astype(BF16)
+        for t in range(rows // TILE):
+            here_too = jnp.where(ids - low == t * TILE, 1.0, 0.0).astype(BF16)
+            acc[pl.ds(t * TILE, TILE), :] += jnp.dot(
+                ones * here_too, got, preferred_element_type=F32
+            )
+
+    wider = [(low, min(low + 2 * PART, messages)) for low in range(0, messages, 2 * PART)]
+    for span in wider[:2]:
         scatter(span)
 
     for step in range(1, groups):
@@ -512,7 +525,7 @@
         def _():
             row_in[chip] = row_out[k]
 
-    for span in spans[3:]:
+    for span in wider[2:]:
         scatter(span)
 
     side = lax.div(me, chips)
@@ -526,23 +539,25 @@
     hub_sum = jnp.sum(row_in[...], axis=0)
     top = hub_sum.astype(BF16).astype(F32)
     both = jnp.concatenate([top, hub_sum - top], axis=0).astype(BF16)
-    hub_ids = meta[pl.ds(3, 1), :][:, : 2 * share]
-
-    def finish(t, _):
-        at = span_of(t)
-        node = lax.broadcasted_iota(I32, (2 * block, 2 * share), 0) + t * (2 * block)
+    hub_ids = hub_ids[:, : 2 * share]
+
+    def result_copy(t):
+        at = pl.ds(t * TILE, TILE)
+        return pltpu.make_async_copy(grad.at[at], grad_hbm.at[at], local.at[13 + t])
+
+    for t in range(rows // TILE):
+        at = pl.ds(t * TILE, TILE)
+        node = lax.broadcasted_iota(I32, (TILE, 2 * share), 0) + t * TILE
         chosen = jnp.where(node == hub_ids, 1.0, 0.0).astype(BF16)
         grad[at, :] = (
             acc[at, :] + jnp.dot(chosen, both, preferred_element_type=F32)
         ).astype(BF16)
-        return _
-
-    lax.fori_loop(0, own_blocks // 2, finish, 0)
+        result_copy(t).start()
 
     for n in range(messages):
         source = here.source(n)
         from_plane(wfin.at[source], f_send.at[n], f_recv.at[source], source).wait_recv()
-    wout[...] = wfin[...]
+    wout_copy = fetch(wfin, wout, 12)
 
     hub_mate.wait_send()
     pair.wait_send()
@@ -561,8 +576,13 @@
         def _():
             row_copy(k).wait_send()
 
-
-def layer_call(meta, lists, features, values, ws, wn, bias, cot, groups, devs, share):
+    for copy in (output_copy, bias_copy, wout_copy):
+        copy.wait()
+    for t in range(rows // TILE):
+        result_copy(t).wait()
+
+
+def layer_call(hub_rows, count, src, tgt, lists, features, values, ws, wn, bias, cot, groups, devs, share):
     own_blocks, block, width = features.shape
     rows = own_blocks * block
     capacity = values.shape[0]
@@ -574,7 +594,7 @@
     dma = pltpu.SemaphoreType.DMA
     vm = pltpu.VMEM
     anywhere = pl.BlockSpec(memory_space=pl.ANY)
-    vmem = pl.BlockSpec(memory_space=pltpu.VMEM)
+    smem = pl.BlockSpec(memory_space=pltpu.SMEM)
     return pl.pallas_call(
         functools.partial(layer_kernel, groups, devs),
         out_shape=(
@@ -583,15 +603,16 @@
             jax.ShapeDtypeStruct((devs, part_rows, width), BF16),
             jax.ShapeDtypeStruct((8, LANES), F32),
         ),
-        in_specs=[anywhere] * 8,
-        out_specs=[vmem] * 4,
+        in_specs=[smem] * 2 + [anywhere] * 9,
+        out_specs=[anywhere] * 4,
         scratch_shapes=[
-            vm(meta.shape, I32), vm(lists.shape, I32),
+            vm(src.shape, I32), vm(tgt.shape, I32), vm((rows, width), BF16), vm((rows, width), BF16),
+            vm((8, LANES), F32), vm((2 * width + 16, rows), BF16), vm(lists.shape, I32),
             vm((capacity + 1, block, block), BF16), vm((capacity + 1, block, block), BF16),
             vm((width, width), BF16), vm((width, width), BF16), vm((1, width), F32),
             vm((rows, width), BF16),
             vm((blocks, block, width), BF16), vm((most + 1, block, width), F32),
-            vm((rows, width), F32), vm((rows, width), BF16), vm((rows, width), BF16),
+            vm((rows, width), F32), vm((rows, width), BF16),
             vm((own_blocks, block, width), BF16), vm((rows, width), F32),
             vm((devs, block, width), BF16), vm((devs, block, width), BF16),
             vm((share, width), F32), vm((2, share, width), F32),
@@ -602,7 +623,7 @@
             vm((devs, part_rows, width + LANES), BF16), vm((devs, part_rows, width + LANES), BF16),
             vm((groups, part_rows, width + LANES), BF16), vm((devs, part_rows, width), BF16),
             vm((2 * ROWS_OF_PLAN, LANES), I32), pltpu.SMEM((2 * ROWS_OF_PLAN, LANES), I32),
-            dma((9,)), dma((devs,)), dma((devs,)), dma((2,)), dma((chips,)), dma((chips,)),
+            dma((13 + rows // TILE,)), dma((devs,)), dma((devs,)), dma((2,)), dma((chips,)), dma((chips,)),
             dma((groups,)), dma((groups,)), dma((groups,)), dma((groups,)),
             dma((devs,)), dma((devs,)), dma((2,)), dma((groups,)), dma((groups,)),
             dma((chips,)), dma((chips,)),
@@ -612,31 +633,70 @@
             collective_id=0, has_side_effects=True, vmem_limit_bytes=56 * MIB
         ),
         name="layer",
-    )(meta, lists, features, values, ws, wn, bias, cot)
+    )(hub_rows, count, src, tgt, lists, features, values, ws, wn, bias, cot)
+
+
+def finish_kernel(
+    scale, output_in, grad_in, weights_in, bias_in,
+    output, grad, grad_self, grad_neigh, grad_bias,
+    weights, sums, self_v, neigh_v, bias_v, sems,
+):
+    def move(src, dst, which):
+        copy = pltpu.make_async_copy(src, dst, sems.at[which])
+        copy.start()
+        return copy
+
+    first = [move(weights_in, weights, 0), move(bias_in, sums, 1)]
+    moved = [move(output_in, output, 2), move(grad_in, grad, 3)]
+    for copy in first:
+        copy.wait()
+    half = weights.shape[0] // 2
+    self_v[...] = weights[pl.ds(0, half)].reshape(self_v.shape).astype(F32) * scale
+    moved.append(move(self_v, grad_self, 0))
+    neigh_v[...] = weights[pl.ds(half, half)].reshape(neigh_v.shape).astype(F32) * scale
+    moved.append(move(neigh_v, grad_neigh, 1))
+    bias_v[...] = jnp.concatenate([sums[pl.ds(0, 1), :], sums[pl.ds(1, 1), :]], axis=1) * scale
+    moved.append(move(bias_v, grad_bias, 4))
+    for copy in moved:
+        copy.wait()
+
+
+def finish_call(scale, output, grad, weights, bias):
+    width = output.shape[1]
+    vm = pltpu.VMEM
+    anywhere = pl.BlockSpec(memory_space=pl.ANY)
+    square = jax.ShapeDtypeStruct((width, width), F32)
+    line = jax.ShapeDtypeStruct((1, width), F32)
+    return pl.pallas_call(
+        functools.partial(finish_kernel, scale),
+        out_shape=(
+            jax.ShapeDtypeStruct(output.shape, BF16), jax.ShapeDtypeStruct(grad.shape, BF16),
+            square, square, line,
+        ),
+        in_specs=[anywhere] * 4,
+        out_specs=[anywhere] * 5,
+        scratch_shapes=[
+            vm(weights.shape, BF16), vm(bias.shape, F32),
+            vm((width, width), F32), vm((width, width), F32), vm((1, width), F32),
+            pltpu.SemaphoreType.DMA((5,)),
+        ],
+        compiler_params=pltpu.CompilerParams(vmem_limit_bytes=63 * MIB),
+        name="finish",
+    )(output, grad, weights, bias)
 
 
 def shards(groups, devs, features, weight_self, weight_neigh, bias, cotangent, hub_rows,
            halo_send, block_src, block_tgt, block_count, block_vals):
     rows, width = features.shape
     scale = 1.0 / math.sqrt(rows * groups * devs)
-    share = hub_rows.shape[0]
     block = block_vals.shape[-1]
-    unused = jnp.full((LANES - 2 * share,), -1, I32)
-    meta = jnp.stack(
-        [
-            block_src[0, 0],
-            block_tgt[0, 0],
-            jnp.broadcast_to(block_count[0, 0], (LANES,)),
-            jnp.concatenate([hub_rows, hub_rows, unused]),
-        ]
+    results = layer_call(
+        hub_rows, block_count, block_src[0], block_tgt[0],
+        halo_send[0, 0], features.reshape(-1, block, width), block_vals[0, 0],
+        weight_self, weight_neigh, bias[None], cotangent, groups, devs, hub_rows.shape[0],
     )
-    meta = jnp.concatenate([meta, jnp.zeros((4, LANES), I32)])
-    output, grad, wout, bias_out = layer_call(
-        meta, halo_send[0, 0], features.reshape(-1, block, width), block_vals[0, 0],
-        weight_self, weight_neigh, bias[None], cotangent, groups, devs, share,
-    )
-    wgrad = wout.reshape(2, width, width).astype(F32) * scale
-    return output, grad, wgrad[0], wgrad[1], bias_out[:2].reshape(width) * scale
+    output, grad, grad_self, grad_neigh, grad_bias = finish_call(scale, *results)
+    return output, grad, grad_self, grad_neigh, grad_bias.reshape(width)
 
 
 def solution(mesh):

time: 97.1 us -> 149 us (1.53)
  Pallas kernels: 87.1 us -> 148 us
  local copies, waits for them, and re-layouts: 5.35 us -> 0 us
  other arithmetic: 3.13 us -> 0 us
    pallas_call x0 -> x1, Pallas kernels: none -> 64.7 us  [finish_call(): pl.pallas_call(functools.partial(finish_kernel, scale), out_shape=(jax.Sh...]
    pallas_call x1, Pallas kernels: 87.1 us -> 83 us  [layer_call(): pl.pallas_call(functools.partial(layer_kernel, groups, devs), out_shape=(...]
    unnamed x4 -> x0, local copies, waits for them, and re-layouts: 3.24 us -> none
    mul x2 -> x0, other arithmetic: 2.32 us -> none  [the longest x1 1.22 us: shards(): bias_out[:2].reshape(width) * scale]
where the time goes in v3:
time: 149 us
  Pallas kernels  148 us (99%)
    pallas_call x1, Pallas kernels, layer_call(): pl.pallas_call(functools.partial(layer_kernel, groups, devs), out_shape=(...  83 us
    pallas_call x1, Pallas kernels, finish_call(): pl.pallas_call(functools.partial(finish_kernel, scale), out_shape=(jax.Sh...  64.7 us

profile of v3, /device:TPU:1, one launch (start us, length us, event | category | flops | bytes accessed | tf_op | source)
XLA Modules:
  0.0 149.2 jit_solution(8505605457681653594)
XLA Ops:
  1.3 83.0 %layer.1 = (bf16[2048,256]{1,0:T(8,128)(2,1)}, bf16[2048,256]{1,0:T(8,128)(2,1)}, bf16[32,16,256]{2,1,0:T(8,128)(2,1)}, f32[8,128]{1,0:T(8,128)}) custom-call(s32[8]{0:T(128)} %hub_rows.1, s32[1,1]{1,0:T(1,128)S(6)} %copy.16.counts, s32[1,128]{1,0:T(1,128)} %bitcast.11, s32[1,128]{1,0:T(1,128)} %bitcast.12, s32[32,128]{1,0:T(8,128)} %bitcast.9, ...), custom_call_target="tpu_custom_call" | custom-call | tf_op jit(solution)/shard_map/layer/pallas_call | solution.py:598
  84.3 64.7 %finish.1 = (bf16[2048,256]{1,0:T(8,128)(2,1)}, bf16[2048,256]{1,0:T(8,128)(2,1)}, f32[256,256]{1,0:T(8,128)}, f32[256,256]{1,0:T(8,128)}, f32[1,256]{1,0:T(1,128)}) custom-call(bf16[2048,256]{1,0:T(8,128)(2,1)} %get-tuple-element.14.output_in, bf16[2048,256]{1,0:T(8,128)(2,1)} %get-tuple-element.15.grad_in, ...), custom_call_target="tpu_custom_call" | custom-call | tf_op jit(solution)/shard_map/finish/pallas_call | solution.py:670

commit v4 on v3

--- a/solution.py
+++ b/solution.py
@@ -27,7 +27,7 @@
 def send_order(devs):
     ys = devs // 8
     every = [(y, x, c) for y in range(ys) for x in range(4) for c in range(2)][1:]
-    draw = random.Random(5)
+    draw = random.Random(1)
     draw.shuffle(every)
     other = [(-y % ys, -x % 4, c) for y, x, c in every]
     return every, other
@@ -109,14 +109,14 @@
     groups, devs,
     hub_rows, counts, src_hbm, tgt_hbm, lists_hbm, feat_hbm, vals_hbm, ws_hbm, wn_hbm, bias_hbm, cot_hbm,
     output_hbm, grad_hbm, wout, bias_out,
-    src_v, tgt_v, output, grad, bias_sum, wide, lists, vals, turned, ws, wn, bias, cot,
+    src_v, tgt_v, output, grad, wide, lists, vals, turned, ws, wn, bias, cot,
     table, runs, own_pre, dpre_ref, dagg, acc,
     halo_out, halo_in, hub_row, hub_pair, hub_send, hub_plane,
-    pair_out, pair_in, z_out, z_in, row_out, row_in, wsend, w_in, wz_in, wfin,
+    pair_out, pair_in, z_out, z_in, row_out, row_in, wsend, wz_in, wmid, w_in, wplane, wall,
     plan_v, plan_s,
     local, h_send, h_recv, m_sem, a_send, a_recv, z_send, z_recv, c_send, c_recv,
     g_send, g_recv, p_sem, s_send, s_recv, r_send, r_recv,
-    w_send, w_recv, y_send, y_recv, f_send, f_recv,
+    w_send, w_recv, y_send, y_recv, f_send, f_recv, u_send, u_recv,
 ):
     group = lax.axis_index("group")
     me = lax.axis_index("dev")
@@ -264,20 +264,37 @@
     both = hub_pair[...].reshape(2 * share, width).astype(BF16)
     hub_send[...] = both
     hub_plane[chip] = both
-    for n in range(1, chips):
-        hub_spread(n).start()
+    spreads = core == lax.div(chip, half_chips)
+
+    @pl.when(spreads)
+    def _():
+        for n in range(1, chips):
+            hub_spread(n).start()
+
     ship(spans[1])
 
     for span in spans[2:]:
         fill(*span)
         ship(span)
 
-    for n in range(1, chips):
-        source = lax.div(here.across(n), 2)
-        from_plane(hub_plane.at[source], a_send.at[n], a_recv.at[source], mate).wait_recv()
+    for n in range(half_chips):
+        source = core * half_chips + n
+
+        @pl.when(source != chip)
+        def _():
+            from_plane(hub_plane.at[source], a_send.at[n], a_recv.at[source], mate).wait_recv()
+
     for step in range(1, groups):
         hub_up(step).start()
-    hub_table[pl.ds(group * chips, chips)] = hub_plane[...]
+    hub_table[pl.ds((group * 2 + core) * half_chips, half_chips)] = hub_plane[
+        pl.ds(core * half_chips, half_chips)
+    ]
+
+    def hub_over(owner):
+        part = hub_in_table(owner, core)
+        return to_plane(part, part, c_send.at[owner], c_recv.at[owner], mate)
+
+    hub_over(group).start()
 
     for copy in late:
         copy.wait()
@@ -285,7 +302,7 @@
     src = src_v[...]
     tgt = tgt_v[...]
     ahead = slot_plan(tgt, src, count, own_blocks)
-    back = slot_plan(src, tgt, count, blocks)
+    back = slot_plan(lax.rem(src + blocks - own_blocks, blocks), tgt, count, blocks)
     for at, row in enumerate(ahead):
         plan_v[pl.ds(at, 1), :] = row
     for at, row in enumerate(back):
@@ -323,15 +340,15 @@
         owner = lax.rem(group + groups - step, groups)
         part = hub_in_table(owner, core)
         to_column(part, part, z_send.at[step], z_recv.at[owner], owner).wait_recv()
-        to_plane(part, part, c_send.at[owner], c_recv.at[owner], mate).start()
+        hub_over(owner).start()
 
     for step in range(1, groups):
         pass_on(step)
 
-    for step in range(1, groups):
+    for step in range(groups):
         owner = lax.rem(group + groups - step, groups)
-        sent, got = hub_in_table(owner, core), hub_in_table(owner, 1 - core)
-        to_plane(sent, sent, c_send.at[owner], c_recv.at[owner], mate).wait_send()
+        got = hub_in_table(owner, 1 - core)
+        hub_over(owner).wait_send()
         to_plane(got, got, c_send.at[owner], c_recv.at[owner], mate).wait_recv()
     for n in range(messages):
         source = here.source(n)
@@ -376,25 +393,23 @@
     lax.fori_loop(0, own_blocks // 4, dense, 0)
     output_copy = fetch(output, output_hbm, 10)
 
-    part_rows = wsend.shape[1]
     sums = jnp.dot(wide[...], dpre_ref[...], preferred_element_type=F32)
-    wsend[:, :, pl.ds(0, width)] = (
-        sums[: 2 * width].astype(BF16).reshape(devs, part_rows, width)
+    pieces, part_rows = wsend.shape[1], wsend.shape[2]
+    wsend[:, pl.ds(0, pieces - 1)] = (
+        sums[: 2 * width].astype(BF16).reshape(groups, pieces - 1, part_rows, width)
     )
-    gbias = sums[2 * width : 2 * width + 1]
-    line = lax.broadcasted_iota(I32, (part_rows, LANES), 0)
-    sums = jnp.where(line == 0, gbias[:, :LANES], jnp.where(line == 1, gbias[:, LANES:], 0.0))
-    wsend[:, :, pl.ds(width, LANES)] = jnp.broadcast_to(
-        sums.astype(BF16)[None], (devs, part_rows, LANES)
+    wsend[:, pieces - 1] = jnp.broadcast_to(
+        sums[2 * width :].astype(BF16)[None], (groups, part_rows, width)
     )
 
-    def w_copy(n):
-        peer = here.target(n)
-        return to_plane(wsend.at[peer], w_in.at[me], w_send.at[n], w_recv.at[me], peer)
-
-    for n in range(messages):
-        w_copy(n).start()
-    w_in[me] = wsend[me]
+    def w_up(step):
+        return to_column(
+            wsend.at[above(step)], wz_in.at[group], y_send.at[step], y_recv.at[group], above(step)
+        )
+
+    for step in range(1, groups):
+        w_up(step).start()
+    wz_in[group] = wsend[group]
     for n in range(messages):
         halo_copy(n).wait_send()
 
@@ -412,38 +427,41 @@
             )
         return _
 
-    lax.fori_loop(0, pl.cdiv(capacity + blocks, 2 * UNROLL), backward, 0)
-
-    def dtable(b):
-        return runs[plan_s[ROWS_OF_PLAN + 5, b]]
+    halo_steps = pl.cdiv(capacity + devs, 2 * UNROLL)
+    lax.fori_loop(0, halo_steps, backward, 0)
+
+    def dtable(key):
+        return runs[plan_s[ROWS_OF_PLAN + 5, key]]
+
+    hub_key, own_key = devs, blocks - own_blocks
 
     def back_copy(n):
         return to_plane(halo_out.at[n], halo_in.at[me], g_send.at[n], g_recv.at[me], here.target(n))
 
     for n in range(messages):
-        halo_out[n] = dtable(own_blocks + here.target(n)).astype(BF16)
+        halo_out[n] = dtable(here.target(n)).astype(BF16)
         back_copy(n).start()
+    lax.fori_loop(halo_steps, pl.cdiv(capacity + blocks, 2 * UNROLL), backward, 0)
     for k in range(groups):
-        pair_out[k] = dtable(hub_start + 2 * k + 1 - core).astype(BF16)
+        pair_out[k] = dtable(hub_key + 2 * k + 1 - core).astype(BF16)
     pair = to_plane(pair_out, pair_in, p_sem.at[0], p_sem.at[1], mate)
     pair.start()
 
-    for n in range(messages):
-        source = here.source(n)
-        from_plane(w_in.at[source], w_send.at[n], w_recv.at[source], source).wait_recv()
-    wz_in[group] = jnp.sum(w_in[...].astype(F32), axis=0).astype(BF16)
-
-    def y_copy(step):
-        return to_column(
-            wz_in.at[group], wz_in.at[group], y_send.at[step], y_recv.at[group], above(step)
-        )
-
-    for step in range(1, groups):
-        y_copy(step).start()
+    def begin(t, _):
+        at = span_of(t)
+        own = jnp.concatenate(
+            [dtable(own_key + t * 2), dtable(own_key + t * 2 + 1)], axis=0
+        )
+        acc[at, :] = own + lax.dot_general(
+            dpre_ref[at, :], ws[...], LAST, preferred_element_type=F32
+        )
+        return _
+
+    lax.fori_loop(0, own_blocks // 2, begin, 0)
 
     pair.wait_recv()
     for k in range(groups):
-        z_out[k] = (dtable(hub_start + 2 * k + core) + pair_in[k].astype(F32)).astype(BF16)
+        z_out[k] = (dtable(hub_key + 2 * k + core) + pair_in[k].astype(F32)).astype(BF16)
 
     def s_copy(step):
         return to_column(
@@ -453,34 +471,39 @@
     for step in range(1, groups):
         s_copy(step).start()
     z_in[group] = z_out[group]
-
-    def begin(t, _):
-        at = span_of(t)
-        own = jnp.concatenate([dtable(t * 2), dtable(t * 2 + 1)], axis=0)
-        acc[at, :] = own + lax.dot_general(
-            dpre_ref[at, :], ws[...], LAST, preferred_element_type=F32
-        )
-        return _
-
-    lax.fori_loop(0, own_blocks // 2, begin, 0)
 
     for step in range(1, groups):
         peer = above(step)
         to_column(
             wz_in.at[peer], wz_in.at[peer], y_send.at[step], y_recv.at[peer], peer
         ).wait_recv()
-    total = jnp.sum(wz_in[...].astype(F32), axis=0)
-    wfin[me] = total[:, :width].astype(BF16)
-    bias_sum[...] = total[:8, width:]
-    bias_copy = fetch(bias_sum, bias_out, 11)
-
-    def f_copy(n):
+    wmid[...] = jnp.sum(wz_in[...].astype(F32), axis=0).astype(BF16)
+    apart = devs // pieces
+    piece = lax.div(me, apart)
+    summing = (lax.rem(me, apart) == 0) & (piece < pieces)
+
+    def w_copy(k):
+        return to_plane(wmid.at[k], w_in.at[me], w_send.at[k], w_recv.at[me], k * apart)
+
+    for k in range(pieces):
+        @pl.when(me != k * apart)
+        def _():
+            w_copy(k).start()
+
+    def w_spread(n):
         return to_plane(
-            wfin.at[me], wfin.at[me], f_send.at[n], f_recv.at[me], here.target(n)
-        )
-
-    for n in range(messages):
-        f_copy(n).start()
+            wplane.at[piece], wplane.at[piece], f_send.at[n], f_recv.at[piece], here.target(n)
+        )
+
+    @pl.when(summing)
+    def _():
+        w_in[me] = wmid[piece]
+        for n in range(messages):
+            source = here.source(n)
+            from_plane(w_in.at[source], f_send.at[n], w_recv.at[source], source).wait_recv()
+        wplane[piece] = jnp.sum(w_in[...].astype(F32), axis=0).astype(BF16)
+        for n in range(messages):
+            w_spread(n).start()
 
     def scatter(span):
         ids, got = [], []
@@ -500,8 +523,9 @@
                 ones * here_too, got, preferred_element_type=F32
             )
 
-    wider = [(low, min(low + 2 * PART, messages)) for low in range(0, messages, 2 * PART)]
-    for span in wider[:2]:
+    edges = [0, 8, 16, 24, 28, messages]
+    wider = list(zip(edges[:-1], edges[1:]))
+    for span in wider[:1]:
         scatter(span)
 
     for step in range(1, groups):
@@ -525,7 +549,23 @@
         def _():
             row_in[chip] = row_out[k]
 
-    for span in wider[2:]:
+    for k in range(pieces):
+        @pl.when(me != k * apart)
+        def _():
+            from_plane(wplane.at[k], f_send.at[k], f_recv.at[k], k * apart).wait_recv()
+
+    def w_around(step):
+        return to_column(
+            wplane.at[pl.ds(0, pieces - 1)], wall.at[group], u_send.at[step], u_recv.at[group],
+            above(step),
+        )
+
+    for step in range(1, groups):
+        w_around(step).start()
+    wall[group] = wplane[pl.ds(0, pieces - 1)]
+    bias_copy = fetch(wplane.at[pieces - 1], bias_out, 11)
+
+    for span in wider[1:]:
         scatter(span)
 
     side = lax.div(me, chips)
@@ -554,23 +594,38 @@
         ).astype(BF16)
         result_copy(t).start()
 
-    for n in range(messages):
-        source = here.source(n)
-        from_plane(wfin.at[source], f_send.at[n], f_recv.at[source], source).wait_recv()
-    wout_copy = fetch(wfin, wout, 12)
+    for step in range(1, groups):
+        peer = above(step)
+        to_column(
+            wall.at[peer], wall.at[peer], u_send.at[step], u_recv.at[peer], peer
+        ).wait_recv()
+    wout_copy = fetch(wall, wout, 12)
 
     hub_mate.wait_send()
     pair.wait_send()
-    for n in range(1, chips):
-        hub_spread(n).wait_send()
+
+    @pl.when(spreads)
+    def _():
+        for n in range(1, chips):
+            hub_spread(n).wait_send()
+
     for step in range(1, groups):
         hub_up(step).wait_send()
-        y_copy(step).wait_send()
+        w_up(step).wait_send()
+        w_around(step).wait_send()
         s_copy(step).wait_send()
     for n in range(messages):
-        w_copy(n).wait_send()
         back_copy(n).wait_send()
-        f_copy(n).wait_send()
+    for k in range(pieces):
+        @pl.when(me != k * apart)
+        def _():
+            w_copy(k).wait_send()
+
+    @pl.when(summing)
+    def _():
+        for n in range(messages):
+            w_spread(n).wait_send()
+
     for k in range(chips):
         @pl.when(core * chips + k != me)
         def _():
@@ -589,7 +644,8 @@
     hubs = groups * devs * share
     blocks = own_blocks + devs + hubs // block
     chips = devs // 2
-    part_rows = 2 * width // devs
+    part_rows = 16
+    pieces = 2 * width // groups // part_rows + 1
     most = UNROLL * pl.cdiv(capacity + blocks, 2 * UNROLL)
     dma = pltpu.SemaphoreType.DMA
     vm = pltpu.VMEM
@@ -600,14 +656,14 @@
         out_shape=(
             jax.ShapeDtypeStruct((rows, width), BF16),
             jax.ShapeDtypeStruct((rows, width), BF16),
-            jax.ShapeDtypeStruct((devs, part_rows, width), BF16),
-            jax.ShapeDtypeStruct((8, LANES), F32),
+            jax.ShapeDtypeStruct((groups, pieces - 1, part_rows, width), BF16),
+            jax.ShapeDtypeStruct((part_rows, width), BF16),
         ),
         in_specs=[smem] * 2 + [anywhere] * 9,
         out_specs=[anywhere] * 4,
         scratch_shapes=[
             vm(src.shape, I32), vm(tgt.shape, I32), vm((rows, width), BF16), vm((rows, width), BF16),
-            vm((8, LANES), F32), vm((2 * width + 16, rows), BF16), vm(lists.shape, I32),
+            vm((2 * width + 16, rows), BF16), vm(lists.shape, I32),
             vm((capacity + 1, block, block), BF16), vm((capacity + 1, block, block), BF16),
             vm((width, width), BF16), vm((width, width), BF16), vm((1, width), F32),
             vm((rows, width), BF16),
@@ -620,14 +676,16 @@
             vm((groups, block, width), BF16), vm((groups, block, width), BF16),
             vm((groups, block, width), BF16), vm((groups, block, width), BF16),
             vm((chips, share, width), F32), vm((chips, share, width), F32),
-            vm((devs, part_rows, width + LANES), BF16), vm((devs, part_rows, width + LANES), BF16),
-            vm((groups, part_rows, width + LANES), BF16), vm((devs, part_rows, width), BF16),
+            vm((groups, pieces, part_rows, width), BF16), vm((groups, pieces, part_rows, width), BF16),
+            vm((pieces, part_rows, width), BF16), vm((devs, part_rows, width), BF16),
+            vm((pieces, part_rows, width), BF16), vm((groups, pieces - 1, part_rows, width), BF16),
             vm((2 * ROWS_OF_PLAN, LANES), I32), pltpu.SMEM((2 * ROWS_OF_PLAN, LANES), I32),
             dma((13 + rows // TILE,)), dma((devs,)), dma((devs,)), dma((2,)), dma((chips,)), dma((chips,)),
             dma((groups,)), dma((groups,)), dma((groups,)), dma((groups,)),
             dma((devs,)), dma((devs,)), dma((2,)), dma((groups,)), dma((groups,)),
             dma((chips,)), dma((chips,)),
-            dma((devs,)), dma((devs,)), dma((groups,)), dma((groups,)), dma((devs,)), dma((devs,)),
+            dma((pieces,)), dma((devs,)), dma((groups,)), dma((groups,)), dma((devs,)), dma((pieces,)),
+            dma((groups,)), dma((groups,)),
         ],
         compiler_params=pltpu.CompilerParams(
             collective_id=0, has_side_effects=True, vmem_limit_bytes=56 * MIB
@@ -639,7 +697,7 @@
 def finish_kernel(
     scale, output_in, grad_in, weights_in, bias_in,
     output, grad, grad_self, grad_neigh, grad_bias,
-    weights, sums, self_v, neigh_v, bias_v, sems,
+    weights, sums, self_v, neigh_v, bias_v, staged, sems,
 ):
     def move(src, dst, which):
         copy = pltpu.make_async_copy(src, dst, sems.at[which])
@@ -647,22 +705,35 @@
         return copy
 
     first = [move(weights_in, weights, 0), move(bias_in, sums, 1)]
-    moved = [move(output_in, output, 2), move(grad_in, grad, 3)]
+    rows = staged.shape[2]
+    whole = [(output_in, output), (grad_in, grad)]
+    pieces = [(which, part) for part in range(staged.shape[1]) for which in range(2)]
+
+    def place(part):
+        return pl.ds(part * rows, rows)
+
+    inward = [
+        move(whole[which][0].at[place(part)], staged.at[which, part], 5 + n)
+        for n, (which, part) in enumerate(pieces)
+    ]
     for copy in first:
         copy.wait()
     half = weights.shape[0] // 2
     self_v[...] = weights[pl.ds(0, half)].reshape(self_v.shape).astype(F32) * scale
-    moved.append(move(self_v, grad_self, 0))
+    moved = [move(self_v, grad_self, 2)]
     neigh_v[...] = weights[pl.ds(half, half)].reshape(neigh_v.shape).astype(F32) * scale
-    moved.append(move(neigh_v, grad_neigh, 1))
-    bias_v[...] = jnp.concatenate([sums[pl.ds(0, 1), :], sums[pl.ds(1, 1), :]], axis=1) * scale
+    moved.append(move(neigh_v, grad_neigh, 3))
+    bias_v[...] = sums[pl.ds(0, 1), :].astype(F32) * scale
     moved.append(move(bias_v, grad_bias, 4))
+    for n, (which, part) in enumerate(pieces):
+        inward[n].wait()
+        moved.append(move(staged.at[which, part], whole[which][1].at[place(part)], 5 + n))
     for copy in moved:
         copy.wait()
 
 
 def finish_call(scale, output, grad, weights, bias):
-    width = output.shape[1]
+    rows, width = output.shape
     vm = pltpu.VMEM
     anywhere = pl.BlockSpec(memory_space=pl.ANY)
     square = jax.ShapeDtypeStruct((width, width), F32)
@@ -676,9 +747,10 @@
         in_specs=[anywhere] * 4,
         out_specs=[anywhere] * 5,
         scratch_shapes=[
-            vm(weights.shape, BF16), vm(bias.shape, F32),
+            vm(weights.shape, BF16), vm(bias.shape, BF16),
             vm((width, width), F32), vm((width, width), F32), vm((1, width), F32),
-            pltpu.SemaphoreType.DMA((5,)),
+            vm((2, rows // TILE, TILE, width), BF16),
+            pltpu.SemaphoreType.DMA((5 + 2 * (rows // TILE),)),
         ],
         compiler_params=pltpu.CompilerParams(vmem_limit_bytes=63 * MIB),
         name="finish",

time: 149 us -> 95.3 us (0.64)
  Pallas kernels: 148 us -> 93.7 us
    pallas_call x1, Pallas kernels: 64.7 us -> 2.57 us  [finish_call(): pl.pallas_call(functools.partial(finish_kernel, scale), out_shape=(jax.Sh...]
    pallas_call x1, Pallas kernels: 83 us -> 91.1 us  [layer_call(): pl.pallas_call(functools.partial(layer_kernel, groups, devs), out_shape=(...]
where the time goes in v4:
time: 95.3 us; the launch traced here: 95.2 us
  Pallas kernels  93.7 us (98%)
  between operations  1.45 us (2%)
    pallas_call x1, Pallas kernels, layer_call(): pl.pallas_call(functools.partial(layer_kernel, groups, devs), out_shape=(...  91.1 us
    pallas_call x1, Pallas kernels, finish_call(): pl.pallas_call(functools.partial(finish_kernel, scale), out_shape=(jax.Sh...  2.57 us

profile of v4, /device:TPU:1, one launch (start us, length us, event | category | flops | bytes accessed | tf_op | source)
XLA Modules:
  0.0 95.2 jit_solution(12564875125402031402)
XLA Ops:
  1.3 91.1 %layer.1 = (bf16[2048,256]{1,0:T(8,128)(2,1)}, bf16[2048,256]{1,0:T(8,128)(2,1)}, bf16[8,4,16,256]{3,2,1,0:T(8,128)(2,1)}, bf16[16,256]{1,0:T(8,128)(2,1)}) custom-call(s32[8]{0:T(128)} %hub_rows.1, s32[1,1]{1,0:T(1,128)S(6)} %copy.16.counts, s32[1,128]{1,0:T(1,128)} %bitcast.11, s32[1,128]{1,0:T(1,128)} %bitcast.12, s32[32,128]{1,0:T(8,128)} %bitcast.9, ...), custom_call_target="tpu_custom_call" | custom-call | tf_op jit(solution)/shard_map/layer/pallas_call | solution.py:654
  92.4 2.6 %finish.1 = (bf16[2048,256]{1,0:T(8,128)(2,1)}, bf16[2048,256]{1,0:T(8,128)(2,1)}, f32[256,256]{1,0:T(8,128)}, f32[256,256]{1,0:T(8,128)}, f32[1,256]{1,0:T(1,128)}) custom-call(bf16[2048,256]{1,0:T(8,128)(2,1)} %get-tuple-element.14.output_in, bf16[2048,256]{1,0:T(8,128)(2,1)} %get-tuple-element.15.grad_in, ...), custom_call_target="tpu_custom_call" | custom-call | tf_op jit(solution)/shard_map/finish/pallas_call | solution.py:741

commit v5 on v4

--- a/solution.py
+++ b/solution.py
@@ -109,14 +109,14 @@
     groups, devs,
     hub_rows, counts, src_hbm, tgt_hbm, lists_hbm, feat_hbm, vals_hbm, ws_hbm, wn_hbm, bias_hbm, cot_hbm,
     output_hbm, grad_hbm, wout, bias_out,
-    src_v, tgt_v, output, grad, wide, lists, vals, turned, ws, wn, bias, cot,
+    src_v, tgt_v, output, grad, bias_sum, wide, lists, vals, turned, ws, wn, bias, cot,
     table, runs, own_pre, dpre_ref, dagg, acc,
     halo_out, halo_in, hub_row, hub_pair, hub_send, hub_plane,
-    pair_out, pair_in, z_out, z_in, row_out, row_in, wsend, wz_in, wmid, w_in, wplane, wall,
+    pair_out, pair_in, z_out, z_in, row_out, row_in, wsend, wmate, wpair, w_in, wz_in, wfin,
     plan_v, plan_s,
     local, h_send, h_recv, m_sem, a_send, a_recv, z_send, z_recv, c_send, c_recv,
     g_send, g_recv, p_sem, s_send, s_recv, r_send, r_recv,
-    w_send, w_recv, y_send, y_recv, f_send, f_recv, u_send, u_recv,
+    w_send, w_recv, y_send, y_recv, f_send, f_recv,
 ):
     group = lax.axis_index("group")
     me = lax.axis_index("dev")
@@ -394,22 +394,18 @@
     output_copy = fetch(output, output_hbm, 10)
 
     sums = jnp.dot(wide[...], dpre_ref[...], preferred_element_type=F32)
-    pieces, part_rows = wsend.shape[1], wsend.shape[2]
-    wsend[:, pl.ds(0, pieces - 1)] = (
-        sums[: 2 * width].astype(BF16).reshape(groups, pieces - 1, part_rows, width)
+    part_rows = wsend.shape[2]
+    wsend[:, :, :, pl.ds(0, width)] = (
+        sums[: 2 * width].astype(BF16).reshape(2, chips, part_rows, width)
     )
-    wsend[:, pieces - 1] = jnp.broadcast_to(
-        sums[2 * width :].astype(BF16)[None], (groups, part_rows, width)
+    line = lax.broadcasted_iota(I32, (part_rows, LANES), 0)
+    gbias = sums[2 * width : 2 * width + 1]
+    gbias = jnp.where(line == 0, gbias[:, :LANES], jnp.where(line == 1, gbias[:, LANES:], 0.0))
+    wsend[:, :, :, pl.ds(width, LANES)] = jnp.broadcast_to(
+        gbias.astype(BF16)[None, None], (2, chips, part_rows, LANES)
     )
-
-    def w_up(step):
-        return to_column(
-            wsend.at[above(step)], wz_in.at[group], y_send.at[step], y_recv.at[group], above(step)
-        )
-
-    for step in range(1, groups):
-        w_up(step).start()
-    wz_in[group] = wsend[group]
+    w_mate = to_plane(wsend.at[1 - core], wmate, m_sem.at[2], m_sem.at[3], mate)
+    w_mate.start()
     for n in range(messages):
         halo_copy(n).wait_send()
 
@@ -428,7 +424,21 @@
         return _
 
     halo_steps = pl.cdiv(capacity + devs, 2 * UNROLL)
-    lax.fori_loop(0, halo_steps, backward, 0)
+    early_steps = halo_steps // 2 - 1
+    lax.fori_loop(0, early_steps, backward, 0)
+    w_mate.wait_recv()
+    wpair[...] = (wsend[core].astype(F32) + wmate[...].astype(F32)).astype(BF16)
+
+    def w_copy(n):
+        target = here.across(n)
+        return to_plane(
+            wpair.at[lax.div(target, 2)], w_in.at[chip], w_send.at[n], w_recv.at[chip], target
+        )
+
+    for n in range(1, chips):
+        w_copy(n).start()
+    w_in[chip] = wpair[chip]
+    lax.fori_loop(early_steps, halo_steps, backward, 0)
 
     def dtable(key):
         return runs[plan_s[ROWS_OF_PLAN + 5, key]]
@@ -447,6 +457,20 @@
     pair = to_plane(pair_out, pair_in, p_sem.at[0], p_sem.at[1], mate)
     pair.start()
 
+    for n in range(1, chips):
+        source = here.across(n)
+        at = lax.div(source, 2)
+        from_plane(w_in.at[at], w_send.at[n], w_recv.at[at], source).wait_recv()
+    wz_in[group] = jnp.sum(w_in[...].astype(F32), axis=0).astype(BF16)
+
+    def y_copy(step):
+        return to_column(
+            wz_in.at[group], wz_in.at[group], y_send.at[step], y_recv.at[group], above(step)
+        )
+
+    for step in range(1, groups):
+        y_copy(step).start()
+
     def begin(t, _):
         at = span_of(t)
         own = jnp.concatenate(
@@ -477,33 +501,17 @@
         to_column(
             wz_in.at[peer], wz_in.at[peer], y_send.at[step], y_recv.at[peer], peer
         ).wait_recv()
-    wmid[...] = jnp.sum(wz_in[...].astype(F32), axis=0).astype(BF16)
-    apart = devs // pieces
-    piece = lax.div(me, apart)
-    summing = (lax.rem(me, apart) == 0) & (piece < pieces)
-
-    def w_copy(k):
-        return to_plane(wmid.at[k], w_in.at[me], w_send.at[k], w_recv.at[me], k * apart)
-
-    for k in range(pieces):
-        @pl.when(me != k * apart)
-        def _():
-            w_copy(k).start()
-
-    def w_spread(n):
-        return to_plane(
-            wplane.at[piece], wplane.at[piece], f_send.at[n], f_recv.at[piece], here.target(n)
-        )
-
-    @pl.when(summing)
-    def _():
-        w_in[me] = wmid[piece]
-        for n in range(messages):
-            source = here.source(n)
-            from_plane(w_in.at[source], f_send.at[n], w_recv.at[source], source).wait_recv()
-        wplane[piece] = jnp.sum(w_in[...].astype(F32), axis=0).astype(BF16)
-        for n in range(messages):
-            w_spread(n).start()
+    total = jnp.sum(wz_in[...].astype(F32), axis=0)
+    wfin[core, chip] = total[:, :width].astype(BF16)
+    bias_sum[...] = total[:8, width:]
+    bias_copy = fetch(bias_sum, bias_out, 11)
+
+    def f_copy(n):
+        part = wfin.at[core, chip]
+        return to_plane(part, part, f_send.at[n], f_recv.at[chip], here.across(n))
+
+    for n in range(1, chips):
+        f_copy(n).start()
 
     def scatter(span):
         ids, got = [], []
@@ -549,23 +557,14 @@
         def _():
             row_in[chip] = row_out[k]
 
-    for k in range(pieces):
-        @pl.when(me != k * apart)
-        def _():
-            from_plane(wplane.at[k], f_send.at[k], f_recv.at[k], k * apart).wait_recv()
-
-    def w_around(step):
-        return to_column(
-            wplane.at[pl.ds(0, pieces - 1)], wall.at[group], u_send.at[step], u_recv.at[group],
-            above(step),
-        )
-
-    for step in range(1, groups):
-        w_around(step).start()
-    wall[group] = wplane[pl.ds(0, pieces - 1)]
-    bias_copy = fetch(wplane.at[pieces - 1], bias_out, 11)
-
-    for span in wider[1:]:
+    scatter(wider[1])
+    for n in range(1, chips):
+        source = here.across(n)
+        at = lax.div(source, 2)
+        from_plane(wfin.at[core, at], f_send.at[n], f_recv.at[at], source).wait_recv()
+    f_mate = to_plane(wfin.at[core], wfin.at[core], m_sem.at[4], m_sem.at[5], mate)
+    f_mate.start()
+    for span in wider[2:]:
         scatter(span)
 
     side = lax.div(me, chips)
@@ -594,12 +593,9 @@
         ).astype(BF16)
         result_copy(t).start()
 
-    for step in range(1, groups):
-        peer = above(step)
-        to_column(
-            wall.at[peer], wall.at[peer], u_send.at[step], u_recv.at[peer], peer
-        ).wait_recv()
-    wout_copy = fetch(wall, wout, 12)
+    other = wfin.at[1 - core]
+    from_plane(other, m_sem.at[4], m_sem.at[5], mate).wait_recv()
+    wout_copy = fetch(wfin, wout, 12)
 
     hub_mate.wait_send()
     pair.wait_send()
@@ -611,21 +607,15 @@
 
     for step in range(1, groups):
         hub_up(step).wait_send()
-        w_up(step).wait_send()
-        w_around(step).wait_send()
+        y_copy(step).wait_send()
         s_copy(step).wait_send()
     for n in range(messages):
         back_copy(n).wait_send()
-    for k in range(pieces):
-        @pl.when(me != k * apart)
-        def _():
-            w_copy(k).wait_send()
-
-    @pl.when(summing)
-    def _():
-        for n in range(messages):
-            w_spread(n).wait_send()
-
+    for n in range(1, chips):
+        w_copy(n).wait_send()
+        f_copy(n).wait_send()
+    w_mate.wait_send()
+    f_mate.wait_send()
     for k in range(chips):
         @pl.when(core * chips + k != me)
         def _():
@@ -644,8 +634,7 @@
     hubs = groups * devs * share
     blocks = own_blocks + devs + hubs // block
     chips = devs // 2
-    part_rows = 16
-    pieces = 2 * width // groups // part_rows + 1
+    part_rows = width // chips
     most = UNROLL * pl.cdiv(capacity + blocks, 2 * UNROLL)
     dma = pltpu.SemaphoreType.DMA
     vm = pltpu.VMEM
@@ -656,14 +645,14 @@
         out_shape=(
             jax.ShapeDtypeStruct((rows, width), BF16),
             jax.ShapeDtypeStruct((rows, width), BF16),
-            jax.ShapeDtypeStruct((groups, pieces - 1, part_rows, width), BF16),
-            jax.ShapeDtypeStruct((part_rows, width), BF16),
+            jax.ShapeDtypeStruct((2, chips, part_rows, width), BF16),
+            jax.ShapeDtypeStruct((8, LANES), F32),
         ),
         in_specs=[smem] * 2 + [anywhere] * 9,
         out_specs=[anywhere] * 4,
         scratch_shapes=[
             vm(src.shape, I32), vm(tgt.shape, I32), vm((rows, width), BF16), vm((rows, width), BF16),
-            vm((2 * width + 16, rows), BF16), vm(lists.shape, I32),
+            vm((8, LANES), F32), vm((2 * width + 16, rows), BF16), vm(lists.shape, I32),
             vm((capacity + 1, block, block), BF16), vm((capacity + 1, block, block), BF16),
             vm((width, width), BF16), vm((width, width), BF16), vm((1, width), F32),
             vm((rows, width), BF16),
@@ -676,16 +665,15 @@
             vm((groups, block, width), BF16), vm((groups, block, width), BF16),
             vm((groups, block, width), BF16), vm((groups, block, width), BF16),
             vm((chips, share, width), F32), vm((chips, share, width), F32),
-            vm((groups, pieces, part_rows, width), BF16), vm((groups, pieces, part_rows, width), BF16),
-            vm((pieces, part_rows, width), BF16), vm((devs, part_rows, width), BF16),
-            vm((pieces, part_rows, width), BF16), vm((groups, pieces - 1, part_rows, width), BF16),
+            vm((2, chips, part_rows, width + LANES), BF16), vm((chips, part_rows, width + LANES), BF16),
+            vm((chips, part_rows, width + LANES), BF16), vm((chips, part_rows, width + LANES), BF16),
+            vm((groups, part_rows, width + LANES), BF16), vm((2, chips, part_rows, width), BF16),
             vm((2 * ROWS_OF_PLAN, LANES), I32), pltpu.SMEM((2 * ROWS_OF_PLAN, LANES), I32),
-            dma((13 + rows // TILE,)), dma((devs,)), dma((devs,)), dma((2,)), dma((chips,)), dma((chips,)),
+            dma((13 + rows // TILE,)), dma((devs,)), dma((devs,)), dma((6,)), dma((chips,)), dma((chips,)),
             dma((groups,)), dma((groups,)), dma((groups,)), dma((groups,)),
             dma((devs,)), dma((devs,)), dma((2,)), dma((groups,)), dma((groups,)),
             dma((chips,)), dma((chips,)),
-            dma((pieces,)), dma((devs,)), dma((groups,)), dma((groups,)), dma((devs,)), dma((pieces,)),
-            dma((groups,)), dma((groups,)),
+            dma((chips,)), dma((chips,)), dma((groups,)), dma((groups,)), dma((chips,)), dma((chips,)),
         ],
         compiler_params=pltpu.CompilerParams(
             collective_id=0, has_side_effects=True, vmem_limit_bytes=56 * MIB
@@ -718,12 +706,11 @@
     ]
     for copy in first:
         copy.wait()
-    half = weights.shape[0] // 2
-    self_v[...] = weights[pl.ds(0, half)].reshape(self_v.shape).astype(F32) * scale
+    self_v[...] = weights[0].reshape(self_v.shape).astype(F32) * scale
     moved = [move(self_v, grad_self, 2)]
-    neigh_v[...] = weights[pl.ds(half, half)].reshape(neigh_v.shape).astype(F32) * scale
+    neigh_v[...] = weights[1].reshape(neigh_v.shape).astype(F32) * scale
     moved.append(move(neigh_v, grad_neigh, 3))
-    bias_v[...] = sums[pl.ds(0, 1), :].astype(F32) * scale
+    bias_v[...] = jnp.concatenate([sums[pl.ds(0, 1), :], sums[pl.ds(1, 1), :]], axis=1) * scale
     moved.append(move(bias_v, grad_bias, 4))
     for n, (which, part) in enumerate(pieces):
         inward[n].wait()
@@ -747,7 +734,7 @@
         in_specs=[anywhere] * 4,
         out_specs=[anywhere] * 5,
         scratch_shapes=[
-            vm(weights.shape, BF16), vm(bias.shape, BF16),
+            vm(weights.shape, BF16), vm(bias.shape, F32),
             vm((width, width), F32), vm((width, width), F32), vm((1, width), F32),
             vm((2, rows // TILE, TILE, width), BF16),
             pltpu.SemaphoreType.DMA((5 + 2 * (rows // TILE),)),

time: 95.3 us -> 86.5 us (0.908)
  Pallas kernels: 93.7 us -> 84.9 us
    pallas_call x1, Pallas kernels: 91.1 us -> 82.3 us  [layer_call(): pl.pallas_call(functools.partial(layer_kernel, groups, devs), out_shape=(...]
where the time goes in v5:
time: 86.5 us; the launch traced here: 86.3 us
  Pallas kernels  84.9 us (98%)
  between operations  1.45 us (2%)
    pallas_call x1, Pallas kernels, layer_call(): pl.pallas_call(functools.partial(layer_kernel, groups, devs), out_shape=(...  82.3 us
    pallas_call x1, Pallas kernels, finish_call(): pl.pallas_call(functools.partial(finish_kernel, scale), out_shape=(jax.Sh...  2.57 us

profile of v5, /device:TPU:1, one launch (start us, length us, event | category | flops | bytes accessed | tf_op | source)
XLA Modules:
  0.0 86.3 jit_solution(2969579119721871112)
XLA Ops:
  1.3 82.3 %layer.1 = (bf16[2048,256]{1,0:T(8,128)(2,1)}, bf16[2048,256]{1,0:T(8,128)(2,1)}, bf16[2,16,16,256]{3,2,1,0:T(8,128)(2,1)}, f32[8,128]{1,0:T(8,128)}) custom-call(s32[8]{0:T(128)} %hub_rows.1, s32[1,1]{1,0:T(1,128)S(6)} %copy.16.counts, s32[1,128]{1,0:T(1,128)} %bitcast.11, s32[1,128]{1,0:T(1,128)} %bitcast.12, s32[32,128]{1,0:T(8,128)} %bitcast.9, ...), custom_call_target="tpu_custom_call" | custom-call | tf_op jit(solution)/shard_map/layer/pallas_call | solution.py:643
  83.6 2.6 %finish.1 = (bf16[2048,256]{1,0:T(8,128)(2,1)}, bf16[2048,256]{1,0:T(8,128)(2,1)}, f32[256,256]{1,0:T(8,128)}, f32[256,256]{1,0:T(8,128)}, f32[1,256]{1,0:T(1,128)}) custom-call(bf16[2048,256]{1,0:T(8,128)(2,1)} %get-tuple-element.14.output_in, bf16[2048,256]{1,0:T(8,128)(2,1)} %get-tuple-element.15.grad_in, ...), custom_call_target="tpu_custom_call" | custom-call | tf_op jit(solution)/shard_map/finish/pallas_call | solution.py:728

commit v6 on v5

--- a/solution.py
+++ b/solution.py
@@ -19,6 +19,8 @@
 MIB = 1 << 20
 PART = 4
 UNROLL = 8
+AHEAD = 24
+BACK = 16
 ROWS_OF_PLAN = 8
 TILE = 512
 LOW = 256
@@ -94,13 +96,12 @@
     left = match & (odds == 0)
     right = match & (odds == 1)
     has_right = total(right)
-    place = along[:1]
     return [
         total(left, down),
         total(right, down) + (1 - has_right) * size,
         total(left, others),
         total(right, others),
-        place * (1 - total(match & (ranks == 0))),
+        1 - total(match & (ranks == 0)),
         total(heads & (keys <= along)) * jnp.minimum(total(live & (keys == along)), 1),
     ]
 
@@ -356,15 +357,26 @@
             table.at[own_blocks + source], h_send.at[n], h_recv.at[source], source
         ).wait_recv()
 
-    def forward(step, _):
-        for u in range(UNROLL):
-            p = step * UNROLL + u
-            left = jnp.concatenate([vals[plan_s[0, p]], vals[plan_s[1, p]]], axis=1)
-            right = jnp.concatenate([table[plan_s[2, p]], table[plan_s[3, p]]], axis=0)
-            runs[p + 1] = runs[plan_s[4, p]] + jnp.dot(left, right, preferred_element_type=F32)
-        return _
-
-    lax.fori_loop(0, pl.cdiv(capacity + own_blocks, 2 * UNROLL), forward, 0)
+    def run_totals(low, high, unroll, start, row, weights, tiles):
+        def body(step, total):
+            for u in range(unroll):
+                p = step * unroll + u
+                left = jnp.concatenate(
+                    [weights[plan_s[row, p]], weights[plan_s[row + 1, p]]], axis=1
+                )
+                right = jnp.concatenate(
+                    [tiles[plan_s[row + 2, p]], tiles[plan_s[row + 3, p]]], axis=0
+                )
+                total = total * plan_s[row + 4, p].astype(F32) + jnp.dot(
+                    left, right, preferred_element_type=F32
+                )
+                runs[p + 1] = total
+            return total
+
+        return lax.fori_loop(low, high, body, start)
+
+    nothing = jnp.zeros((block, width), F32)
+    run_totals(0, pl.cdiv(capacity + own_blocks, 2 * AHEAD), AHEAD, nothing, 0, vals, table)
 
     def dense_part(t):
         at = span_of(t)
@@ -386,11 +398,11 @@
         )
 
     def dense(step, _):
-        dense_part(step * 2)
-        dense_part(step * 2 + 1)
+        for u in range(4):
+            dense_part(step * 4 + u)
         return _
 
-    lax.fori_loop(0, own_blocks // 4, dense, 0)
+    lax.fori_loop(0, own_blocks // 8, dense, 0)
     output_copy = fetch(output, output_hbm, 10)
 
     sums = jnp.dot(wide[...], dpre_ref[...], preferred_element_type=F32)
@@ -409,23 +421,12 @@
     for n in range(messages):
         halo_copy(n).wait_send()
 
-    def backward(step, _):
-        for u in range(UNROLL):
-            p = step * UNROLL + u
-            left = jnp.concatenate(
-                [turned[plan_s[ROWS_OF_PLAN, p]], turned[plan_s[ROWS_OF_PLAN + 1, p]]], axis=1
-            )
-            right = jnp.concatenate(
-                [dagg[plan_s[ROWS_OF_PLAN + 2, p]], dagg[plan_s[ROWS_OF_PLAN + 3, p]]], axis=0
-            )
-            runs[p + 1] = runs[plan_s[ROWS_OF_PLAN + 4, p]] + jnp.dot(
-                left, right, preferred_element_type=F32
-            )
-        return _
-
-    halo_steps = pl.cdiv(capacity + devs, 2 * UNROLL)
-    early_steps = halo_steps // 2 - 1
-    lax.fori_loop(0, early_steps, backward, 0)
+    def backward(low, high, start):
+        return run_totals(low, high, BACK, start, ROWS_OF_PLAN, turned, dagg)
+
+    halo_steps = pl.cdiv(capacity + devs, 2 * BACK)
+    early_steps = halo_steps // 2
+    reached = backward(0, early_steps, nothing)
     w_mate.wait_recv()
     wpair[...] = (wsend[core].astype(F32) + wmate[...].astype(F32)).astype(BF16)
 
@@ -438,7 +439,7 @@
     for n in range(1, chips):
         w_copy(n).start()
     w_in[chip] = wpair[chip]
-    lax.fori_loop(early_steps, halo_steps, backward, 0)
+    reached = backward(early_steps, halo_steps, reached)
 
     def dtable(key):
         return runs[plan_s[ROWS_OF_PLAN + 5, key]]
@@ -451,7 +452,7 @@
     for n in range(messages):
         halo_out[n] = dtable(here.target(n)).astype(BF16)
         back_copy(n).start()
-    lax.fori_loop(halo_steps, pl.cdiv(capacity + blocks, 2 * UNROLL), backward, 0)
+    backward(halo_steps, pl.cdiv(capacity + blocks, 2 * BACK), reached)
     for k in range(groups):
         pair_out[k] = dtable(hub_key + 2 * k + 1 - core).astype(BF16)
     pair = to_plane(pair_out, pair_in, p_sem.at[0], p_sem.at[1], mate)
@@ -635,7 +636,9 @@
     blocks = own_blocks + devs + hubs // block
     chips = devs // 2
     part_rows = width // chips
-    most = UNROLL * pl.cdiv(capacity + blocks, 2 * UNROLL)
+    most = max(
+        AHEAD * pl.cdiv(capacity + own_blocks, 2 * AHEAD), BACK * pl.cdiv(capacity + blocks, 2 * BACK)
+    )
     dma = pltpu.SemaphoreType.DMA
     vm = pltpu.VMEM
     anywhere = pl.BlockSpec(memory_space=pl.ANY)

time: 86.5 us -> 83.9 us (0.970)
  Pallas kernels: 84.9 us -> 82.4 us
    pallas_call x1, Pallas kernels: 82.3 us -> 79.8 us  [layer_call(): pl.pallas_call(functools.partial(layer_kernel, groups, devs), out_shape=(...]
where the time goes in v6:
time: 83.9 us; the launch traced here: 83.8 us
  Pallas kernels  82.4 us (98%)
  between operations  1.45 us (2%)
    pallas_call x1, Pallas kernels, layer_call(): pl.pallas_call(functools.partial(layer_kernel, groups, devs), out_shape=(...  79.8 us
    pallas_call x1, Pallas kernels, finish_call(): pl.pallas_call(functools.partial(finish_kernel, scale), out_shape=(jax.Sh...  2.57 us

profile of v6, /device:TPU:1, one launch (start us, length us, event | category | flops | bytes accessed | tf_op | source)
XLA Modules:
  0.0 83.8 jit_solution(777393212325799537)
XLA Ops:
  1.3 79.8 %layer.1 = (bf16[2048,256]{1,0:T(8,128)(2,1)}, bf16[2048,256]{1,0:T(8,128)(2,1)}, bf16[2,16,16,256]{3,2,1,0:T(8,128)(2,1)}, f32[8,128]{1,0:T(8,128)}) custom-call(s32[8]{0:T(128)} %hub_rows.1, s32[1,1]{1,0:T(1,128)S(6)} %copy.16.counts, s32[1,128]{1,0:T(1,128)} %bitcast.11, s32[1,128]{1,0:T(1,128)} %bitcast.12, s32[32,128]{1,0:T(8,128)} %bitcast.9, ...), custom_call_target="tpu_custom_call" | custom-call | tf_op jit(solution)/shard_map/layer/pallas_call | solution.py:646
  81.1 2.6 %finish.1 = (bf16[2048,256]{1,0:T(8,128)(2,1)}, bf16[2048,256]{1,0:T(8,128)(2,1)}, f32[256,256]{1,0:T(8,128)}, f32[256,256]{1,0:T(8,128)}, f32[1,256]{1,0:T(1,128)}) custom-call(bf16[2048,256]{1,0:T(8,128)(2,1)} %get-tuple-element.14.output_in, bf16[2048,256]{1,0:T(8,128)(2,1)} %get-tuple-element.15.grad_in, ...), custom_call_target="tpu_custom_call" | custom-call | tf_op jit(solution)/shard_map/finish/pallas_call | solution.py:731

commit v7 on v6

--- a/solution.py
+++ b/solution.py
@@ -112,7 +112,7 @@
     output_hbm, grad_hbm, wout, bias_out,
     src_v, tgt_v, output, grad, bias_sum, wide, lists, vals, turned, ws, wn, bias, cot,
     table, runs, own_pre, dpre_ref, dagg, acc,
-    halo_out, halo_in, hub_row, hub_pair, hub_send, hub_plane,
+    halo_out, halo_back, halo_in, hub_row, hub_pair, hub_send, hub_plane,
     pair_out, pair_in, z_out, z_in, row_out, row_in, wsend, wmate, wpair, w_in, wz_in, wfin,
     plan_v, plan_s,
     local, h_send, h_recv, m_sem, a_send, a_recv, z_send, z_recv, c_send, c_recv,
@@ -166,6 +166,8 @@
         pl.semaphore_signal(
             barrier, inc=1, device_id={"group": above(step)}, device_id_type=MESH
         )
+    for copy in early:
+        copy.wait()
     late = [
         fetch(vals_hbm, vals.at[pl.ds(0, capacity)], 3),
         fetch(ws_hbm, ws, 4),
@@ -175,8 +177,6 @@
         fetch(src_hbm, src_v, 2),
         fetch(tgt_hbm, tgt_v, 9),
     ]
-    for copy in early:
-        copy.wait()
 
     lane = lax.broadcasted_iota(I32, (block, LANES), 1)
     owned = pl.ds(0, own_blocks)
@@ -200,13 +200,6 @@
     def pick(matrix):
         return jnp.dot(matrix, table[owned].reshape(rows, width), preferred_element_type=F32)
 
-    hub_ids = jnp.full((1, block), rows, I32)
-    for k in range(share):
-        hub_ids = jnp.where((lane[:1] == k) | (lane[:1] == k + share), hub_rows[k], hub_ids)
-    picked = pick(onehot(column_of(hub_ids, block)[: 2 * share]))[:share]
-    hub_row[...] = picked
-    hub_pair[core] = picked
-
     def fill(low, high):
         parts = [
             onehot(column_of(lists[pl.ds(here.target(n), 1), :], block))
@@ -223,7 +216,8 @@
     def from_plane(dst, send, recv, peer):
         return to_plane(dst, dst, send, recv, peer)
 
-    spans = [(low, min(low + PART, messages)) for low in range(0, messages, PART)]
+    starts = [0, 2] + list(range(2 + PART, messages, PART))
+    spans = list(zip(starts, starts[1:] + [messages]))
 
     def ship(span):
         for n in range(*span):
@@ -257,8 +251,14 @@
 
     fill(*spans[0])
     pl.semaphore_wait(barrier, devs + groups - 2)
+    ship(spans[0])
+    hub_ids = jnp.full((1, block), rows, I32)
+    for k in range(share):
+        hub_ids = jnp.where((lane[:1] == k) | (lane[:1] == k + share), hub_rows[k], hub_ids)
+    picked = pick(onehot(column_of(hub_ids, block)[: 2 * share]))[:share]
+    hub_row[...] = picked
+    hub_pair[core] = picked
     hub_mate.start()
-    ship(spans[0])
     fill(*spans[1])
 
     hub_mate.wait_recv()
@@ -418,9 +418,6 @@
     )
     w_mate = to_plane(wsend.at[1 - core], wmate, m_sem.at[2], m_sem.at[3], mate)
     w_mate.start()
-    for n in range(messages):
-        halo_copy(n).wait_send()
-
     def backward(low, high, start):
         return run_totals(low, high, BACK, start, ROWS_OF_PLAN, turned, dagg)
 
@@ -447,10 +444,10 @@
     hub_key, own_key = devs, blocks - own_blocks
 
     def back_copy(n):
-        return to_plane(halo_out.at[n], halo_in.at[me], g_send.at[n], g_recv.at[me], here.target(n))
+        return to_plane(halo_back.at[n], halo_in.at[me], g_send.at[n], g_recv.at[me], here.target(n))
 
     for n in range(messages):
-        halo_out[n] = dtable(here.target(n)).astype(BF16)
+        halo_back[n] = dtable(here.target(n)).astype(BF16)
         back_copy(n).start()
     backward(halo_steps, pl.cdiv(capacity + blocks, 2 * BACK), reached)
     for k in range(groups):
@@ -484,6 +481,8 @@
 
     lax.fori_loop(0, own_blocks // 2, begin, 0)
 
+    for n in range(messages):
+        halo_copy(n).wait_send()
     pair.wait_recv()
     for k in range(groups):
         z_out[k] = (dtable(hub_key + 2 * k + core) + pair_in[k].astype(F32)).astype(BF16)
@@ -514,8 +513,12 @@
     for n in range(1, chips):
         f_copy(n).start()
 
-    def scatter(span):
-        ids, got = [], []
+    def result_copy(t):
+        at = pl.ds(t * TILE, TILE)
+        return pltpu.make_async_copy(grad.at[at], grad_hbm.at[at], local.at[13 + t])
+
+    def scatter(span, more_ids=(), more=(), last=False):
+        ids, got = list(more_ids), list(more)
         for n in range(*span):
             source = here.source(n)
             from_plane(halo_in.at[source], g_send.at[n], g_recv.at[source], source).wait_recv()
@@ -528,9 +531,13 @@
         ones = jnp.where(node == low, 1.0, 0.0).astype(BF16)
         for t in range(rows // TILE):
             here_too = jnp.where(ids - low == t * TILE, 1.0, 0.0).astype(BF16)
-            acc[pl.ds(t * TILE, TILE), :] += jnp.dot(
-                ones * here_too, got, preferred_element_type=F32
-            )
+            at = pl.ds(t * TILE, TILE)
+            added = acc[at, :] + jnp.dot(ones * here_too, got, preferred_element_type=F32)
+            if last:
+                grad[at, :] = added.astype(BF16)
+                result_copy(t).start()
+            else:
+                acc[at, :] = added
 
     edges = [0, 8, 16, 24, 28, messages]
     wider = list(zip(edges[:-1], edges[1:]))
@@ -565,7 +572,7 @@
         from_plane(wfin.at[core, at], f_send.at[n], f_recv.at[at], source).wait_recv()
     f_mate = to_plane(wfin.at[core], wfin.at[core], m_sem.at[4], m_sem.at[5], mate)
     f_mate.start()
-    for span in wider[2:]:
+    for span in wider[2:-1]:
         scatter(span)
 
     side = lax.div(me, chips)
@@ -578,25 +585,8 @@
 
     hub_sum = jnp.sum(row_in[...], axis=0)
     top = hub_sum.astype(BF16).astype(F32)
-    both = jnp.concatenate([top, hub_sum - top], axis=0).astype(BF16)
-    hub_ids = hub_ids[:, : 2 * share]
-
-    def result_copy(t):
-        at = pl.ds(t * TILE, TILE)
-        return pltpu.make_async_copy(grad.at[at], grad_hbm.at[at], local.at[13 + t])
-
-    for t in range(rows // TILE):
-        at = pl.ds(t * TILE, TILE)
-        node = lax.broadcasted_iota(I32, (TILE, 2 * share), 0) + t * TILE
-        chosen = jnp.where(node == hub_ids, 1.0, 0.0).astype(BF16)
-        grad[at, :] = (
-            acc[at, :] + jnp.dot(chosen, both, preferred_element_type=F32)
-        ).astype(BF16)
-        result_copy(t).start()
-
-    other = wfin.at[1 - core]
-    from_plane(other, m_sem.at[4], m_sem.at[5], mate).wait_recv()
-    wout_copy = fetch(wfin, wout, 12)
+    spare = jnp.zeros((block - 2 * share, width), F32)
+    both = jnp.concatenate([top, hub_sum - top, spare], axis=0).astype(BF16)
 
     hub_mate.wait_send()
     pair.wait_send()
@@ -610,8 +600,6 @@
         hub_up(step).wait_send()
         y_copy(step).wait_send()
         s_copy(step).wait_send()
-    for n in range(messages):
-        back_copy(n).wait_send()
     for n in range(1, chips):
         w_copy(n).wait_send()
         f_copy(n).wait_send()
@@ -622,6 +610,15 @@
         def _():
             row_copy(k).wait_send()
 
+    other = wfin.at[1 - core]
+    from_plane(other, m_sem.at[4], m_sem.at[5], mate).wait_recv()
+    wout_copy = fetch(wfin, wout, 12)
+    for n in range(wider[-2][0]):
+        back_copy(n).wait_send()
+
+    scatter(wider[-1], [hub_ids], [both], last=True)
+    for n in range(wider[-2][0], messages):
+        back_copy(n).wait_send()
     for copy in (output_copy, bias_copy, wout_copy):
         copy.wait()
     for t in range(rows // TILE):
@@ -662,7 +659,7 @@
             vm((blocks, block, width), BF16), vm((most + 1, block, width), F32),
             vm((rows, width), F32), vm((rows, width), BF16),
             vm((own_blocks, block, width), BF16), vm((rows, width), F32),
-            vm((devs, block, width), BF16), vm((devs, block, width), BF16),
+            vm((devs, block, width), BF16), vm((devs, block, width), BF16), vm((devs, block, width), BF16),
             vm((share, width), F32), vm((2, share, width), F32),
             vm((2 * share, width), BF16), vm((chips, 2 * share, width), BF16),
             vm((groups, block, width), BF16), vm((groups, block, width), BF16),

time: 83.9 us -> 84.1 us (level)
  no operation moved by 1% of the time
where the time goes in v7:
time: 84.1 us; the launch traced here: 84 us
  Pallas kernels  82.5 us (98%)
  between operations  1.45 us (2%)
    pallas_call x1, Pallas kernels, layer_call(): pl.pallas_call(functools.partial(layer_kernel, groups, devs), out_shape=(...  80 us
    pallas_call x1, Pallas kernels, finish_call(): pl.pallas_call(functools.partial(finish_kernel, scale), out_shape=(jax.Sh...  2.57 us

profile of v7, /device:TPU:1, one launch (start us, length us, event | category | flops | bytes accessed | tf_op | source)
XLA Modules:
  0.0 84.0 jit_solution(17481293740440942806)
XLA Ops:
  1.3 80.0 %layer.1 = (bf16[2048,256]{1,0:T(8,128)(2,1)}, bf16[2048,256]{1,0:T(8,128)(2,1)}, bf16[2,16,16,256]{3,2,1,0:T(8,128)(2,1)}, f32[8,128]{1,0:T(8,128)}) custom-call(s32[8]{0:T(128)} %hub_rows.1, s32[1,1]{1,0:T(1,128)S(6)} %copy.16.counts, s32[1,128]{1,0:T(1,128)} %bitcast.11, s32[1,128]{1,0:T(1,128)} %bitcast.12, s32[32,128]{1,0:T(8,128)} %bitcast.9, ...), custom_call_target="tpu_custom_call" | custom-call | tf_op jit(solution)/shard_map/layer/pallas_call | solution.py:643
  81.3 2.6 %finish.1 = (bf16[2048,256]{1,0:T(8,128)(2,1)}, bf16[2048,256]{1,0:T(8,128)(2,1)}, f32[256,256]{1,0:T(8,128)}, f32[256,256]{1,0:T(8,128)}, f32[1,256]{1,0:T(1,128)}) custom-call(bf16[2048,256]{1,0:T(8,128)(2,1)} %get-tuple-element.14.output_in, bf16[2048,256]{1,0:T(8,128)(2,1)} %get-tuple-element.15.grad_in, ...), custom_call_target="tpu_custom_call" | custom-call | tf_op jit(solution)/shard_map/finish/pallas_call | solution.py:728

commit v8 on v7

--- a/solution.py
+++ b/solution.py
@@ -405,6 +405,29 @@
     lax.fori_loop(0, own_blocks // 8, dense, 0)
     output_copy = fetch(output, output_hbm, 10)
 
+    def backward(low, high, start):
+        return run_totals(low, high, BACK, start, ROWS_OF_PLAN, turned, dagg)
+
+    halo_steps = pl.cdiv(capacity + devs, 2 * BACK)
+    reached = backward(0, halo_steps, nothing)
+
+    def dtable(key):
+        return runs[plan_s[ROWS_OF_PLAN + 5, key]]
+
+    hub_key, own_key = devs, blocks - own_blocks
+
+    def back_copy(n):
+        return to_plane(halo_back.at[n], halo_in.at[me], g_send.at[n], g_recv.at[me], here.target(n))
+
+    for n in range(messages):
+        halo_back[n] = dtable(here.target(n)).astype(BF16)
+        back_copy(n).start()
+    backward(halo_steps, pl.cdiv(capacity + blocks, 2 * BACK), reached)
+    for k in range(groups):
+        pair_out[k] = dtable(hub_key + 2 * k + 1 - core).astype(BF16)
+    pair = to_plane(pair_out, pair_in, p_sem.at[0], p_sem.at[1], mate)
+    pair.start()
+
     sums = jnp.dot(wide[...], dpre_ref[...], preferred_element_type=F32)
     part_rows = wsend.shape[2]
     wsend[:, :, :, pl.ds(0, width)] = (
@@ -418,12 +441,31 @@
     )
     w_mate = to_plane(wsend.at[1 - core], wmate, m_sem.at[2], m_sem.at[3], mate)
     w_mate.start()
-    def backward(low, high, start):
-        return run_totals(low, high, BACK, start, ROWS_OF_PLAN, turned, dagg)
-
-    halo_steps = pl.cdiv(capacity + devs, 2 * BACK)
-    early_steps = halo_steps // 2
-    reached = backward(0, early_steps, nothing)
+    def begin(t, _):
+        at = span_of(t)
+        own = jnp.concatenate(
+            [dtable(own_key + t * 2), dtable(own_key + t * 2 + 1)], axis=0
+        )
+        acc[at, :] = own + lax.dot_general(
+            dpre_ref[at, :], ws[...], LAST, preferred_element_type=F32
+        )
+        return _
+
+    lax.fori_loop(0, own_blocks // 2, begin, 0)
+
+    pair.wait_recv()
+    for k in range(groups):
+        z_out[k] = (dtable(hub_key + 2 * k + core) + pair_in[k].astype(F32)).astype(BF16)
+
+    def s_copy(step):
+        return to_column(
+            z_out.at[above(step)], z_in.at[group], s_send.at[step], s_recv.at[group], above(step)
+        )
+
+    for step in range(1, groups):
+        s_copy(step).start()
+    z_in[group] = z_out[group]
+
     w_mate.wait_recv()
     wpair[...] = (wsend[core].astype(F32) + wmate[...].astype(F32)).astype(BF16)
 
@@ -436,24 +478,9 @@
     for n in range(1, chips):
         w_copy(n).start()
     w_in[chip] = wpair[chip]
-    reached = backward(early_steps, halo_steps, reached)
-
-    def dtable(key):
-        return runs[plan_s[ROWS_OF_PLAN + 5, key]]
-
-    hub_key, own_key = devs, blocks - own_blocks
-
-    def back_copy(n):
-        return to_plane(halo_back.at[n], halo_in.at[me], g_send.at[n], g_recv.at[me], here.target(n))
 
     for n in range(messages):
-        halo_back[n] = dtable(here.target(n)).astype(BF16)
-        back_copy(n).start()
-    backward(halo_steps, pl.cdiv(capacity + blocks, 2 * BACK), reached)
-    for k in range(groups):
-        pair_out[k] = dtable(hub_key + 2 * k + 1 - core).astype(BF16)
-    pair = to_plane(pair_out, pair_in, p_sem.at[0], p_sem.at[1], mate)
-    pair.start()
+        halo_copy(n).wait_send()
 
     for n in range(1, chips):
         source = here.across(n)
@@ -469,32 +496,6 @@
     for step in range(1, groups):
         y_copy(step).start()
 
-    def begin(t, _):
-        at = span_of(t)
-        own = jnp.concatenate(
-            [dtable(own_key + t * 2), dtable(own_key + t * 2 + 1)], axis=0
-        )
-        acc[at, :] = own + lax.dot_general(
-            dpre_ref[at, :], ws[...], LAST, preferred_element_type=F32
-        )
-        return _
-
-    lax.fori_loop(0, own_blocks // 2, begin, 0)
-
-    for n in range(messages):
-        halo_copy(n).wait_send()
-    pair.wait_recv()
-    for k in range(groups):
-        z_out[k] = (dtable(hub_key + 2 * k + core) + pair_in[k].astype(F32)).astype(BF16)
-
-    def s_copy(step):
-        return to_column(
-            z_out.at[above(step)], z_in.at[group], s_send.at[step], s_recv.at[group], above(step)
-        )
-
-    for step in range(1, groups):
-        s_copy(step).start()
-    z_in[group] = z_out[group]
 
     for step in range(1, groups):
         peer = above(step)
@@ -541,9 +542,6 @@
 
     edges = [0, 8, 16, 24, 28, messages]
     wider = list(zip(edges[:-1], edges[1:]))
-    for span in wider[:1]:
-        scatter(span)
-
     for step in range(1, groups):
         peer = above(step)
         to_column(
@@ -565,7 +563,8 @@
         def _():
             row_in[chip] = row_out[k]
 
-    scatter(wider[1])
+    for span in wider[:2]:
+        scatter(span)
     for n in range(1, chips):
         source = here.across(n)
         at = lax.div(source, 2)

time: 84.1 us -> 92.8 us (1.10)
  Pallas kernels: 82.5 us -> 91.2 us
    pallas_call x1, Pallas kernels: 80 us -> 88.6 us  [layer_call(): pl.pallas_call(functools.partial(layer_kernel, groups, devs), out_shape=(...]
where the time goes in v8:
time: 92.8 us; the launch traced here: 92.6 us
  Pallas kernels  91.2 us (98%)
  between operations  1.45 us (2%)
    pallas_call x1, Pallas kernels, layer_call(): pl.pallas_call(functools.partial(layer_kernel, groups, devs), out_shape=(...  88.6 us
    pallas_call x1, Pallas kernels, finish_call(): pl.pallas_call(functools.partial(finish_kernel, scale), out_shape=(jax.Sh...  2.57 us

profile of v8, /device:TPU:1, one launch (start us, length us, event | category | flops | bytes accessed | tf_op | source)
XLA Modules:
  0.0 92.6 jit_solution(416551003430429874)
XLA Ops:
  1.3 88.6 %layer.1 = (bf16[2048,256]{1,0:T(8,128)(2,1)}, bf16[2048,256]{1,0:T(8,128)(2,1)}, bf16[2,16,16,256]{3,2,1,0:T(8,128)(2,1)}, f32[8,128]{1,0:T(8,128)}) custom-call(s32[8]{0:T(128)} %hub_rows.1, s32[1,1]{1,0:T(1,128)S(6)} %copy.16.counts, s32[1,128]{1,0:T(1,128)} %bitcast.11, s32[1,128]{1,0:T(1,128)} %bitcast.12, s32[32,128]{1,0:T(8,128)} %bitcast.9, ...), custom_call_target="tpu_custom_call" | custom-call | tf_op jit(solution)/shard_map/layer/pallas_call | solution.py:642
  89.9 2.6 %finish.1 = (bf16[2048,256]{1,0:T(8,128)(2,1)}, bf16[2048,256]{1,0:T(8,128)(2,1)}, f32[256,256]{1,0:T(8,128)}, f32[256,256]{1,0:T(8,128)}, f32[1,256]{1,0:T(1,128)}) custom-call(bf16[2048,256]{1,0:T(8,128)(2,1)} %get-tuple-element.14.output_in, bf16[2048,256]{1,0:T(8,128)(2,1)} %get-tuple-element.15.grad_in, ...), custom_call_target="tpu_custom_call" | custom-call | tf_op jit(solution)/shard_map/finish/pallas_call | solution.py:727
